TPU v7x, 32 devices: a whole 2x2x4 slice. The times are simulated.
32 devices in a mesh: dp: 16 (over z, y, x), rep: 2 (over core).
Axes of the slice: x: 2, y: 2, z: 4, core: 2. Of those that a mesh axis runs over, the one named last changes fastest.
Arguments:
- language_in: bfloat16 [64, 128, 768], P(('dp', 'rep')), may hold values from -6 to 6
- vision_in: bfloat16 [64, 128, 768], P(('dp', 'rep')), may hold values from -6 to 6
- language_count: int32 [64], P(('dp', 'rep')), may hold values from 5 to 128, as said below
- vision_count: int32 [64], P(('dp', 'rep')), may hold values from 5 to 128, as said below
- cross_qkv: bfloat16 [2, 3, 768, 768], P(None, None, 'dp'), may hold values from -0.21875 to 0.21875
- cross_proj: bfloat16 [2, 768, 768], P(None, 'dp'), may hold values from -1.25 to 1.25
- cross_bias: bfloat16 [2, 3, 768], P(None, None, 'dp'), may hold values from -4 to 4
- norm_gain: bfloat16 [2, 3, 768], P(None, None, 'dp'), may hold values from 0.5 to 1.5
- norm_bias: bfloat16 [2, 3, 768], P(None, None, 'dp'), may hold values from -4 to 4
- self_qkv: bfloat16 [2, 3, 768, 768], P(None, None, 'dp'), may hold values from -0.21875 to 0.21875
- self_proj: bfloat16 [2, 768, 768], P(None, 'dp'), may hold values from -1.25 to 1.25
- self_bias: bfloat16 [2, 3, 768], P(None, None, 'dp'), may hold values from -4 to 4
- ffn_in: bfloat16 [2, 768, 3072], P(None, 'dp'), may hold values from -0.21875 to 0.21875
- ffn_in_bias: bfloat16 [2, 3072], P(None, 'dp'), may hold values from -4 to 4
- ffn_out: bfloat16 [2, 3072, 768], P(None, 'dp'), may hold values from -0.109375 to 0.109375
- ffn_out_bias: bfloat16 [2, 768], P(None, 'dp'), may hold values from -4 to 4
- gate_weight: bfloat16 [2, 768, 768], P(None, 'dp'), may hold values from -0.15625 to 0.15625
- gate_bias: bfloat16 [768], P('dp'), may hold values from -6 to 6
- cotangent: bfloat16 [64, 128, 768], P(('dp', 'rep')), may hold values from -6 to 6
Outputs:
- united: bfloat16 [64, 128, 768], P(('dp', 'rep'))
- grad_language: bfloat16 [64, 128, 768], P(('dp', 'rep'))
- grad_vision: bfloat16 [64, 128, 768], P(('dp', 'rep'))
- grad_cross_qkv: float32 [2, 3, 768, 768], P(None, None, 'dp')
- grad_cross_proj: float32 [2, 768, 768], P(None, 'dp')
- grad_cross_bias: float32 [2, 3, 768], P(None, None, 'dp')
- grad_norm_gain: float32 [2, 3, 768], P(None, None, 'dp')
- grad_norm_bias: float32 [2, 3, 768], P(None, None, 'dp')
- grad_self_qkv: float32 [2, 3, 768, 768], P(None, None, 'dp')
- grad_self_proj: float32 [2, 768, 768], P(None, 'dp')
- grad_self_bias: float32 [2, 3, 768], P(None, None, 'dp')
- grad_ffn_in: float32 [2, 768, 3072], P(None, 'dp')
- grad_ffn_in_bias: float32 [2, 3072], P(None, 'dp')
- grad_ffn_out: float32 [2, 3072, 768], P(None, 'dp')
- grad_ffn_out_bias: float32 [2, 768], P(None, 'dp')
- grad_gate_weight: float32 [2, 768, 768], P(None, 'dp')
- grad_gate_bias: float32 [768], P('dp')
Inputs may be any that keep to these rules, and one draw needn't show every extreme that they name: The real language regions of a page are its first language_count slots. The real vision regions of a page are its first vision_count slots.
All inputs are finite; a program needn't handle non-finite values.
Results may differ from a plain program's by a relative error of at most 0.024.
Values may be sent and summed in bfloat16 or wider, within the bound.
No kernel may reach another device: no remote copies, remote signals or barrier semaphores. Data moves between devices by JAX's collectives and lax.ppermute only.
A program may use at most 256 MiB of HBM per device.

v0:
```python
import jax
import jax.numpy as jnp
from jax import lax
from jax.sharding import PartitionSpec as P

HEADS = 12
HEAD = 64


norm_epsilon = 1e-05


def project(values, weight):
    return jnp.einsum("spnd,sde->spne", values, weight, preferred_element_type=jnp.float32)


def project_back(grads_low, weight):
    return jnp.einsum("spne,sde->spnd", grads_low, weight, preferred_element_type=jnp.float32)


def weight_grad(values, grads_low):
    return jnp.einsum("spnd,spne->sde", values, grads_low, preferred_element_type=jnp.float32)


def bias_grad(grads_low):
    return jnp.sum(grads_low.astype(jnp.float32), axis=(1, 2))


def widened(bias):
    return bias.astype(jnp.float32)[:, None, None, :]


def layer_norm(values, scale_row, shift_row):
    mean_row = jnp.mean(values, axis=-1, keepdims=True)
    centred = values - mean_row
    variance = jnp.mean(centred * centred, axis=-1, keepdims=True)
    return (
        centred * lax.rsqrt(variance + norm_epsilon) * scale_row[:, None, None, :]
        + shift_row[:, None, None, :]
    )


def gelu_tanh(values):
    return (
        0.5
        * values
        * (1.0 + jnp.tanh(0.7978845608028654 * (values + 0.044715 * values * values * values)))
    )


def split_heads(values):
    return values.reshape(values.shape[:3] + (HEADS, HEAD))


def masked_scores(queries, keys, counts):
    raw_scores = jnp.einsum(
        "spnhk,spmhk->sphnm",
        split_heads(queries),
        split_heads(keys),
        preferred_element_type=jnp.float32,
    ) * HEAD ** (-0.5)
    valid_keys = (
        jnp.arange(keys.shape[2])[None, None, None, None, :] < counts[:, :, None, None, None]
    )
    return jnp.where(valid_keys, raw_scores, -1000000000.0)


def attend_forward(queries, keys, values, counts):
    scores = masked_scores(queries, keys, counts)
    peak_score = jnp.max(scores, axis=-1, keepdims=True)
    log_total = peak_score + jnp.log(jnp.sum(jnp.exp(scores - peak_score), axis=-1, keepdims=True))
    soft_low = jnp.exp(scores - log_total).astype(jnp.bfloat16)
    mixed_heads = jnp.einsum(
        "sphnm,spmhk->spnhk", soft_low, split_heads(values), preferred_element_type=jnp.float32
    )
    return (mixed_heads.reshape(queries.shape).astype(jnp.bfloat16), log_total)


def attend_backward(queries, keys, values, counts, log_total, grad_mixed):
    scores = masked_scores(queries, keys, counts)
    softened = jnp.exp(scores - log_total)
    grad_heads = split_heads(grad_mixed)
    grad_values = jnp.einsum(
        "sphnm,spnhk->spmhk",
        softened.astype(jnp.bfloat16),
        grad_heads,
        preferred_element_type=jnp.float32,
    )
    grad_soft = jnp.einsum(
        "spnhk,spmhk->sphnm", grad_heads, split_heads(values), preferred_element_type=jnp.float32
    )
    grad_scores = (
        softened * (grad_soft - jnp.sum(softened * grad_soft, axis=-1, keepdims=True))
    ).astype(jnp.bfloat16)
    grad_queries = jnp.einsum(
        "sphnm,spmhk->spnhk", grad_scores, split_heads(keys), preferred_element_type=jnp.float32
    ) * HEAD ** (-0.5)
    grad_keys = jnp.einsum(
        "sphnm,spnhk->spmhk", grad_scores, split_heads(queries), preferred_element_type=jnp.float32
    ) * HEAD ** (-0.5)
    layout = queries.shape
    return (
        grad_queries.reshape(layout).astype(jnp.bfloat16),
        grad_keys.reshape(layout).astype(jnp.bfloat16),
        grad_values.reshape(layout).astype(jnp.bfloat16),
    )


def block_forward(source, others, counts, weights, biases, projection):
    queries = (project(source, weights[:, 0]) + widened(biases[:, 0])).astype(jnp.bfloat16)
    keys = project(others, weights[:, 1]).astype(jnp.bfloat16)
    values = (project(others, weights[:, 2]) + widened(biases[:, 1])).astype(jnp.bfloat16)
    mixed, log_total = attend_forward(queries, keys, values, counts)
    output = project(mixed, projection) + widened(biases[:, 2])
    return (output, (queries, keys, values, mixed, log_total))


def block_backward(source, others, counts, weights, projection, saved, grad_output):
    queries, keys, values, mixed, log_total = saved
    grad_low = grad_output.astype(jnp.bfloat16)
    grad_projection = weight_grad(mixed, grad_low)
    grad_mixed = project_back(grad_low, projection).astype(jnp.bfloat16)
    grad_queries, grad_keys, grad_values = attend_backward(
        queries, keys, values, counts, log_total, grad_mixed
    )
    grad_weights = jnp.stack(
        [
            weight_grad(source, grad_queries),
            weight_grad(others, grad_keys),
            weight_grad(others, grad_values),
        ],
        axis=1,
    )
    grad_biases = jnp.stack(
        [bias_grad(grad_queries), bias_grad(grad_values), bias_grad(grad_low)], axis=1
    )
    grad_source = project_back(grad_queries, weights[:, 0])
    grad_others = project_back(grad_keys, weights[:, 1]) + project_back(grad_values, weights[:, 2])
    return (grad_source, grad_others, grad_weights, grad_projection, grad_biases)


def on_device(
    language_in,
    vision_in,
    language_count,
    vision_count,
    cross_qkv,
    cross_proj,
    cross_bias,
    norm_gain,
    norm_bias,
    self_qkv,
    self_proj,
    self_bias,
    ffn_in,
    ffn_in_bias,
    ffn_out,
    ffn_out_bias,
    gate_weight,
    gate_bias,
    cotangent,
):
    cross_full = (
        lax.all_gather(cross_qkv, "dp", axis=2, tiled=True),
        lax.all_gather(cross_proj, "dp", axis=1, tiled=True),
        lax.all_gather(cross_bias, "dp", axis=2, tiled=True),
    )
    rest_full = (
        lax.all_gather(self_qkv, "dp", axis=2, tiled=True),
        lax.all_gather(self_proj, "dp", axis=1, tiled=True),
        lax.all_gather(self_bias, "dp", axis=2, tiled=True),
        lax.all_gather(norm_gain, "dp", axis=2, tiled=True),
        lax.all_gather(norm_bias, "dp", axis=2, tiled=True),
        lax.all_gather(ffn_in, "dp", axis=1, tiled=True),
        lax.all_gather(ffn_in_bias, "dp", axis=1, tiled=True),
        lax.all_gather(ffn_out, "dp", axis=1, tiled=True),
        lax.all_gather(ffn_out_bias, "dp", axis=1, tiled=True),
        lax.all_gather(gate_weight, "dp", axis=1, tiled=True),
        lax.all_gather(gate_bias, "dp", axis=0, tiled=True),
    )
    inputs = jnp.stack([language_in, vision_in])
    counts = jnp.stack([language_count, vision_count])
    others = inputs[::-1]
    other_counts = counts[::-1]
    cross_weights, cross_projection, cross_biases = cross_full
    (
        self_weights,
        self_projection,
        self_biases,
        gains_full,
        shifts_full,
        ffn_in_full,
        ffn_in_bias_full,
        ffn_out_full,
        ffn_out_bias_full,
        gate_full,
        gate_bias_full,
    ) = rest_full
    gains_float = gains_full.astype(jnp.float32)
    shifts_float = shifts_full.astype(jnp.float32)
    cross_out, unused_saved = block_forward(
        inputs, others, other_counts, cross_weights, cross_biases, cross_projection
    )
    first_sum = inputs.astype(jnp.float32) + cross_out
    first_norm = layer_norm(first_sum, gains_float[:, 0], shifts_float[:, 0])
    first_low = first_norm.astype(jnp.bfloat16)
    inner_out, inner_saved = block_forward(
        first_low, first_low, counts, self_weights, self_biases, self_projection
    )
    second_sum = first_norm + inner_out
    second_norm = layer_norm(second_sum, gains_float[:, 1], shifts_float[:, 1])
    second_low = second_norm.astype(jnp.bfloat16)
    hidden = project(second_low, ffn_in_full) + widened(ffn_in_bias_full)
    active_low = gelu_tanh(hidden).astype(jnp.bfloat16)
    branch = project(active_low, ffn_out_full) + widened(ffn_out_bias_full)
    third_sum = second_norm + branch
    third_norm = layer_norm(third_sum, gains_float[:, 2], shifts_float[:, 2])
    third_low = third_norm.astype(jnp.bfloat16)
    logits = jnp.einsum(
        "spnd,sde->pne", third_low, gate_full, preferred_element_type=jnp.float32
    ) + gate_bias_full.astype(jnp.float32)
    mixing = 1.0 / (1.0 + jnp.exp(-logits))
    united_out = mixing * third_norm[0] + (1.0 - mixing) * third_norm[1]
    rest_back = (
        lax.all_gather(self_qkv, "dp", axis=2, tiled=True),
        lax.all_gather(self_proj, "dp", axis=1, tiled=True),
        lax.all_gather(self_bias, "dp", axis=2, tiled=True),
        lax.all_gather(norm_gain, "dp", axis=2, tiled=True),
        lax.all_gather(norm_bias, "dp", axis=2, tiled=True),
        lax.all_gather(ffn_in, "dp", axis=1, tiled=True),
        lax.all_gather(ffn_in_bias, "dp", axis=1, tiled=True),
        lax.all_gather(ffn_out, "dp", axis=1, tiled=True),
        lax.all_gather(ffn_out_bias, "dp", axis=1, tiled=True),
        lax.all_gather(gate_weight, "dp", axis=1, tiled=True),
        lax.all_gather(gate_bias, "dp", axis=0, tiled=True),
    )
    (
        self_weights_back,
        self_projection_back,
        unused_self_bias,
        gains_back,
        shifts_back,
        ffn_in_back,
        unused_in_bias,
        ffn_out_back,
        unused_out_bias,
        gate_back,
        unused_gate_bias,
    ) = rest_back
    gains_back_float = gains_back.astype(jnp.float32)
    shifts_back_float = shifts_back.astype(jnp.float32)
    grad_united = cotangent.astype(jnp.float32)
    grad_logits_low = (
        grad_united * (third_norm[0] - third_norm[1]) * mixing * (1.0 - mixing)
    ).astype(jnp.bfloat16)
    grad_gate = jnp.einsum(
        "spnd,pne->sde", third_low, grad_logits_low, preferred_element_type=jnp.float32
    )
    grad_gate_bias = jnp.sum(grad_logits_low.astype(jnp.float32), axis=(0, 1))
    grad_third = jnp.stack([grad_united * mixing, grad_united * (1.0 - mixing)]) + jnp.einsum(
        "pne,sde->spnd", grad_logits_low, gate_back, preferred_element_type=jnp.float32
    )
    unused_third, third_pull = jax.vjp(
        layer_norm, third_sum, gains_back_float[:, 2], shifts_back_float[:, 2]
    )
    grad_third_sum, grad_gain_third, grad_shift_third = third_pull(grad_third)
    grad_branch_low = grad_third_sum.astype(jnp.bfloat16)
    grad_ffn_out = weight_grad(active_low, grad_branch_low)
    grad_ffn_out_bias = bias_grad(grad_branch_low)
    grad_active = project_back(grad_branch_low, ffn_out_back)
    unused_active, gelu_pull = jax.vjp(gelu_tanh, hidden)
    grad_hidden_low = gelu_pull(grad_active)[0].astype(jnp.bfloat16)
    grad_ffn_in = weight_grad(second_low, grad_hidden_low)
    grad_ffn_in_bias = bias_grad(grad_hidden_low)
    grad_second = grad_third_sum + project_back(grad_hidden_low, ffn_in_back)
    unused_second, second_pull = jax.vjp(
        layer_norm, second_sum, gains_back_float[:, 1], shifts_back_float[:, 1]
    )
    grad_second_sum, grad_gain_second, grad_shift_second = second_pull(grad_second)
    (
        grad_self_source,
        grad_self_others,
        grad_self_weights,
        grad_self_projection,
        grad_self_biases,
    ) = block_backward(
        first_low,
        first_low,
        counts,
        self_weights_back,
        self_projection_back,
        inner_saved,
        grad_second_sum,
    )
    grad_first = grad_second_sum + grad_self_source + grad_self_others
    unused_first, first_pull = jax.vjp(
        layer_norm, first_sum, gains_back_float[:, 0], shifts_back_float[:, 0]
    )
    grad_first_sum, grad_gain_first, grad_shift_first = first_pull(grad_first)
    cross_back = (
        lax.all_gather(cross_qkv, "dp", axis=2, tiled=True),
        lax.all_gather(cross_proj, "dp", axis=1, tiled=True),
        lax.all_gather(cross_bias, "dp", axis=2, tiled=True),
    )
    cross_weights_back, cross_projection_back, cross_biases_back = cross_back
    unused_cross, cross_saved = block_forward(
        inputs, others, other_counts, cross_weights_back, cross_biases_back, cross_projection_back
    )
    (
        grad_cross_source,
        grad_cross_others,
        grad_cross_weights,
        grad_cross_projection,
        grad_cross_biases,
    ) = block_backward(
        inputs,
        others,
        other_counts,
        cross_weights_back,
        cross_projection_back,
        cross_saved,
        grad_first_sum,
    )
    grad_inputs = grad_first_sum + grad_cross_source + grad_cross_others[::-1]
    grad_gains = jnp.stack([grad_gain_first, grad_gain_second, grad_gain_third], axis=1)
    grad_shifts = jnp.stack([grad_shift_first, grad_shift_second, grad_shift_third], axis=1)
    scattered = (
        lax.psum_scatter(grad_cross_weights, "dp", scatter_dimension=2, tiled=True),
        lax.psum_scatter(grad_cross_projection, "dp", scatter_dimension=1, tiled=True),
        lax.psum_scatter(grad_cross_biases, "dp", scatter_dimension=2, tiled=True),
        lax.psum_scatter(grad_gains, "dp", scatter_dimension=2, tiled=True),
        lax.psum_scatter(grad_shifts, "dp", scatter_dimension=2, tiled=True),
        lax.psum_scatter(grad_self_weights, "dp", scatter_dimension=2, tiled=True),
        lax.psum_scatter(grad_self_projection, "dp", scatter_dimension=1, tiled=True),
        lax.psum_scatter(grad_self_biases, "dp", scatter_dimension=2, tiled=True),
        lax.psum_scatter(grad_ffn_in, "dp", scatter_dimension=1, tiled=True),
        lax.psum_scatter(grad_ffn_in_bias, "dp", scatter_dimension=1, tiled=True),
        lax.psum_scatter(grad_ffn_out, "dp", scatter_dimension=1, tiled=True),
        lax.psum_scatter(grad_ffn_out_bias, "dp", scatter_dimension=1, tiled=True),
        lax.psum_scatter(grad_gate, "dp", scatter_dimension=1, tiled=True),
        lax.psum_scatter(grad_gate_bias, "dp", scatter_dimension=0, tiled=True),
    )
    bias_twice = jnp.stack([scattered[13], scattered[13]])
    halves = (
        lax.psum_scatter(
            scattered[0].astype(jnp.bfloat16), "rep", scatter_dimension=0, tiled=True
        ).astype(jnp.float32),
        lax.psum_scatter(
            scattered[1].astype(jnp.bfloat16), "rep", scatter_dimension=0, tiled=True
        ).astype(jnp.float32),
        lax.psum_scatter(
            scattered[2].astype(jnp.bfloat16), "rep", scatter_dimension=0, tiled=True
        ).astype(jnp.float32),
        lax.psum_scatter(
            scattered[3].astype(jnp.bfloat16), "rep", scatter_dimension=0, tiled=True
        ).astype(jnp.float32),
        lax.psum_scatter(
            scattered[4].astype(jnp.bfloat16), "rep", scatter_dimension=0, tiled=True
        ).astype(jnp.float32),
        lax.psum_scatter(
            scattered[5].astype(jnp.bfloat16), "rep", scatter_dimension=0, tiled=True
        ).astype(jnp.float32),
        lax.psum_scatter(
            scattered[6].astype(jnp.bfloat16), "rep", scatter_dimension=0, tiled=True
        ).astype(jnp.float32),
        lax.psum_scatter(
            scattered[7].astype(jnp.bfloat16), "rep", scatter_dimension=0, tiled=True
        ).astype(jnp.float32),
        lax.psum_scatter(
            scattered[8].astype(jnp.bfloat16), "rep", scatter_dimension=0, tiled=True
        ).astype(jnp.float32),
        lax.psum_scatter(
            scattered[9].astype(jnp.bfloat16), "rep", scatter_dimension=0, tiled=True
        ).astype(jnp.float32),
        lax.psum_scatter(
            scattered[10].astype(jnp.bfloat16), "rep", scatter_dimension=0, tiled=True
        ).astype(jnp.float32),
        lax.psum_scatter(
            scattered[11].astype(jnp.bfloat16), "rep", scatter_dimension=0, tiled=True
        ).astype(jnp.float32),
        lax.psum_scatter(
            scattered[12].astype(jnp.bfloat16), "rep", scatter_dimension=0, tiled=True
        ).astype(jnp.float32),
        lax.psum_scatter(
            bias_twice.astype(jnp.bfloat16), "rep", scatter_dimension=0, tiled=True
        ).astype(jnp.float32),
    )
    joined = (
        lax.all_gather(halves[0].astype(jnp.bfloat16), "rep", axis=0, tiled=True).astype(
            jnp.float32
        ),
        lax.all_gather(halves[1].astype(jnp.bfloat16), "rep", axis=0, tiled=True).astype(
            jnp.float32
        ),
        lax.all_gather(halves[2].astype(jnp.bfloat16), "rep", axis=0, tiled=True).astype(
            jnp.float32
        ),
        lax.all_gather(halves[3].astype(jnp.bfloat16), "rep", axis=0, tiled=True).astype(
            jnp.float32
        ),
        lax.all_gather(halves[4].astype(jnp.bfloat16), "rep", axis=0, tiled=True).astype(
            jnp.float32
        ),
        lax.all_gather(halves[5].astype(jnp.bfloat16), "rep", axis=0, tiled=True).astype(
            jnp.float32
        ),
        lax.all_gather(halves[6].astype(jnp.bfloat16), "rep", axis=0, tiled=True).astype(
            jnp.float32
        ),
        lax.all_gather(halves[7].astype(jnp.bfloat16), "rep", axis=0, tiled=True).astype(
            jnp.float32
        ),
        lax.all_gather(halves[8].astype(jnp.bfloat16), "rep", axis=0, tiled=True).astype(
            jnp.float32
        ),
        lax.all_gather(halves[9].astype(jnp.bfloat16), "rep", axis=0, tiled=True).astype(
            jnp.float32
        ),
        lax.all_gather(halves[10].astype(jnp.bfloat16), "rep", axis=0, tiled=True).astype(
            jnp.float32
        ),
        lax.all_gather(halves[11].astype(jnp.bfloat16), "rep", axis=0, tiled=True).astype(
            jnp.float32
        ),
        lax.all_gather(halves[12].astype(jnp.bfloat16), "rep", axis=0, tiled=True).astype(
            jnp.float32
        ),
    )
    return (
        (
            united_out.astype(jnp.bfloat16),
            grad_inputs[0].astype(jnp.bfloat16),
            grad_inputs[1].astype(jnp.bfloat16),
        )
        + tuple(joined)
        + (halves[13][0],)
    )


def solution(mesh):
    return jax.shard_map(
        on_device,
        mesh=mesh,
        in_specs=(
            P(("dp", "rep"), None, None),
            P(("dp", "rep"), None, None),
            P(("dp", "rep")),
            P(("dp", "rep")),
            P(None, None, "dp", None),
            P(None, "dp", None),
            P(None, None, "dp"),
            P(None, None, "dp"),
            P(None, None, "dp"),
            P(None, None, "dp", None),
            P(None, "dp", None),
            P(None, None, "dp"),
            P(None, "dp", None),
            P(None, "dp"),
            P(None, "dp", None),
            P(None, "dp"),
            P(None, "dp", None),
            P("dp"),
            P(("dp", "rep"), None, None),
        ),
        out_specs=(
            P(("dp", "rep"), None, None),
            P(("dp", "rep"), None, None),
            P(("dp", "rep"), None, None),
            P(None, None, "dp", None),
            P(None, "dp", None),
            P(None, None, "dp"),
            P(None, None, "dp"),
            P(None, None, "dp"),
            P(None, None, "dp", None),
            P(None, "dp", None),
            P(None, None, "dp"),
            P(None, "dp", None),
            P(None, "dp"),
            P(None, "dp", None),
            P(None, "dp"),
            P(None, "dp", None),
            P("dp"),
        ),
        check_vma=False,
    )
```

profile of v0, /device:TPU:0, one launch (start us, length us, event | category | flops | bytes accessed | tf_op | source)
XLA Modules:
  0.0 2979.7 jit_solution(10838973805113956159)
XLA Ops:
  17.3 44.2 %all-reduce = bf16[768]{0:T(1024)(128)(2,1)S(1)} all-reduce(bf16[768]{0:T(1024)(128)(2,1)S(1)} %dynamic-update-slice), channel_id=1, replica_groups=mesh['dp'=16,'rep'=2] {'dp'}, use_global_device_ids=true, to_apply=%add | all-reduce | flops 768 | bytes 3072
  62.0 35.7 %all-gather.1 = bf16[16,48,2]{1,2,0:T(2,128)(2,1)S(1)} all-gather(bf16[1,48,2]{1,2,0:T(2,128)(2,1)S(1)} %bitcast.492), channel_id=1, replica_groups=mesh['dp'=16,'rep'=2] {'dp'}, dimensions={0}, use_global_device_ids=true | all-gather | bytes 3264 | tf_op jit(solution)/shard_map/all_gather | solution.py:177
  98.4 37.3 %all-gather = bf16[16,192,2]{1,2,0:T(2,128)(2,1)S(1)} all-gather(bf16[1,192,2]{1,2,0:T(2,128)(2,1)S(1)} %bitcast.490), channel_id=1, replica_groups=mesh['dp'=16,'rep'=2] {'dp'}, dimensions={0}, use_global_device_ids=true | all-gather | bytes 13056 | tf_op jit(solution)/shard_map/all_gather | solution.py:175
  137.0 39.2 %all_gather.96 = bf16[2,3,768]{1,0,2:T(2,128)(2,1)S(1)} all-gather(bf16[2,3,48]{1,0,2:T(2,128)(2,1)S(1)} %copy.289), channel_id=1, replica_groups=mesh['dp'=16,'rep'=2] {'dp'}, dimensions={2}, use_global_device_ids=true | all-gather | bytes 9792 | tf_op jit(solution)/shard_map/all_gather | solution.py:171
  176.2 40.5 %all_gather.94 = bf16[2,3,768]{1,0,2:T(2,128)(2,1)S(1)} all-gather(bf16[2,3,48]{1,0,2:T(2,128)(2,1)S(1)} %copy.286), channel_id=1, replica_groups=mesh['dp'=16,'rep'=2] {'dp'}, dimensions={2}, use_global_device_ids=true | all-gather | bytes 9792 | tf_op jit(solution)/shard_map/all_gather | solution.py:173
  216.7 40.2 %all_gather.93 = bf16[2,3,768]{1,0,2:T(2,128)(2,1)S(1)} all-gather(bf16[2,3,48]{1,0,2:T(2,128)(2,1)S(1)} %copy.284), channel_id=1, replica_groups=mesh['dp'=16,'rep'=2] {'dp'}, dimensions={2}, use_global_device_ids=true | all-gather | bytes 9792 | tf_op jit(solution)/shard_map/all_gather | solution.py:172
  256.9 42.8 %all_gather.91 = bf16[2,3,768]{1,0,2:T(2,128)(2,1)S(1)} all-gather(bf16[2,3,48]{1,0,2:T(2,128)(2,1)S(1)} %copy.275), channel_id=1, replica_groups=mesh['dp'=16,'rep'=2] {'dp'}, dimensions={2}, use_global_device_ids=true | all-gather | bytes 9792 | tf_op jit(solution)/shard_map/all_gather | solution.py:166
  322.1 3.6 add_convert_fusion.4
  327.3 3.6 add_convert_fusion.3
  352.2 3.3 add_convert_fusion.2
  361.5 3.7 fusion.124
  365.6 116.6 %all-gather.20.cloned.1.call-done = bf16[2,768,3072]{2,1,0:T(8,128)(2,1)} async-done(((bf16[2,48,3072]{2,1,0:T(8,128)(2,1)}), bf16[2,768,3072]{2,1,0:T(8,128)(2,1)}) %all-gather.20.cloned.1.call-update) | async-done | bytes 9437200 | tf_op jit(solution)/shard_map/all_gather | solution.py:174
  482.2 8.4 fusion.2
  490.6 114.8 %all-gather.22.cloned.1.call-done = bf16[2,3072,768]{2,1,0:T(8,128)(2,1)} async-done(((bf16[2,192,768]{2,1,0:T(8,128)(2,1)}), bf16[2,3072,768]{2,1,0:T(8,128)(2,1)}) %all-gather.22.cloned.1.call-update) | async-done | bytes 9437200 | tf_op jit(solution)/shard_map/all_gather | solution.py:176
  605.4 8.7 fusion.125
  615.6 53.1 %all-gather.24.cloned.1.call-done = bf16[2,768,768]{2,1,0:T(8,128)(2,1)} async-done(((bf16[2,48,768]{2,1,0:T(8,128)(2,1)}), bf16[2,768,768]{2,1,0:T(8,128)(2,1)}) %all-gather.24.cloned.1.call-update) | async-done | bytes 2359312 | tf_op jit(solution)/shard_map/all_gather | solution.py:178
  668.7 4.6 convert_reduce_fusion.8
  676.3 4.4 multiply_reduce_fusion.2
  682.2 11.9 convert_reduce_fusion
  694.1 8.7 multiply_reduce_fusion.3
  735.4 3.8 fusion.60
  750.1 3.2 convolution_bitcast_fusion.10
  759.4 12.0 pad_maximum_fusion
  772.8 3.2 convolution_bitcast_fusion.5
  776.0 3.1 convolution_bitcast_fusion.6
  779.1 3.1 convolution_bitcast_fusion.4
  782.2 12.0 pad_maximum_fusion.1
  795.3 12.6 convolution_bitcast_fusion
  820.8 9.9 convolution_bitcast_fusion.1
  832.6 122.7 %reduce-scatter.39.cloned.1.call-done = f32[2,48,768]{2,1,0:T(8,128)} async-done(((f32[2,768,768]{2,1,0:T(8,128)}), f32[2,48,768]{2,1,0:T(8,128)}) %reduce-scatter.39.cloned.1.call-update) | async-done | bytes 294928 | tf_op jit(solution)/shard_map/reduce_scatter | solution.py:329
  957.0 139.9 %reduce-scatter.45.cloned.1.call-done = f32[2,48,768]{2,1,0:T(8,128)} async-done(((f32[2,768,768]{2,1,0:T(8,128)}), f32[2,48,768]{2,1,0:T(8,128)}) %reduce-scatter.45.cloned.1.call-update) | async-done | bytes 294928 | tf_op jit(solution)/shard_map/reduce_scatter | solution.py:334
  1098.6 225.5 %reduce-scatter.37.cloned.1.call-done = f32[2,3,48,768]{3,2,0,1:T(8,128)} async-done(((f32[2,3,768,768]{3,2,0,1:T(8,128)}), f32[2,3,48,768]{3,2,0,1:T(8,128)}) %reduce-scatter.37.cloned.1.call-update) | async-done | bytes 884752 | tf_op jit(solution)/shard_map/reduce_scatter | solution.py:328
  1326.1 224.6 %reduce-scatter.43.cloned.1.call-done = f32[2,3,48,768]{3,2,0,1:T(8,128)} async-done(((f32[2,3,768,768]{3,2,0,1:T(8,128)}), f32[2,3,48,768]{3,2,0,1:T(8,128)}) %reduce-scatter.43.cloned.1.call-update) | async-done | bytes 884752 | tf_op jit(solution)/shard_map/reduce_scatter | solution.py:333
  1554.1 42.1 %all-reduce.9 = bf16[768]{0:T(1024)(128)(2,1)S(1)} all-reduce(f32[768]{0:T(1024)S(1)} %copy-done.103), channel_id=28, replica_groups=mesh['dp'=16,'rep'=2] {'dp'}, use_global_device_ids=true, to_apply=%region_59.60.clone | all-reduce | flops 768 | bytes 4608
  1596.3 3.7 fusion.30
  1600.0 243.4 %reduce-scatter.53.cloned.1.call-done = f32[2,192,768]{2,1,0:T(8,128)} async-done(((f32[2,3072,768]{2,1,0:T(8,128)}), f32[2,192,768]{2,1,0:T(8,128)}) %reduce-scatter.53.cloned.1.call-update) | async-done | bytes 1179664 | tf_op jit(solution)/shard_map/reduce_scatter | solution.py:338
  1845.7 3.2 fusion.46
  1852.4 117.0 %reduce-scatter.71.cloned.1.call-done = f32[48,2]{1,0:T(8,128)} async-done(((f32[768,2]{1,0:T(8,128)}), f32[48,2]{1,0:T(8,128)}) %reduce-scatter.71.cloned.1.call-update) | async-done | bytes 400
  1970.2 124.5 %reduce-scatter.67.cloned.1.call-done = f32[48,6]{1,0:T(8,128)} async-done(((f32[768,6]{1,0:T(8,128)}), f32[48,6]{1,0:T(8,128)}) %reduce-scatter.67.cloned.1.call-update) | async-done | bytes 1168
  2095.7 125.0 %reduce-scatter.65.cloned.1.call-done = f32[48,6]{1,0:T(8,128)} async-done(((f32[768,6]{1,0:T(8,128)}), f32[48,6]{1,0:T(8,128)}) %reduce-scatter.65.cloned.1.call-update) | async-done | bytes 1168
  2221.6 124.3 %reduce-scatter.63.cloned.1.call-done = f32[48,6]{1,0:T(8,128)} async-done(((f32[768,6]{1,0:T(8,128)}), f32[48,6]{1,0:T(8,128)}) %reduce-scatter.63.cloned.1.call-update) | async-done | bytes 1168
  2346.9 125.0 %reduce-scatter.61.cloned.1.call-done = f32[48,6]{1,0:T(8,128)} async-done(((f32[768,6]{1,0:T(8,128)}), f32[48,6]{1,0:T(8,128)}) %reduce-scatter.61.cloned.1.call-update) | async-done | bytes 1168
  2472.9 127.5 %reduce-scatter.69.cloned.1.call-done = f32[192,2]{1,0:T(8,128)} async-done(((f32[3072,2]{1,0:T(8,128)}), f32[192,2]{1,0:T(8,128)}) %reduce-scatter.69.cloned.1.call-update) | async-done | bytes 1552
  2601.4 3.3 all-reduce.11
  2606.0 284.2 %reduce-scatter.49.cloned.1.call-done = f32[2,48,3072]{2,1,0:T(8,128)} async-done(((f32[2,768,3072]{2,1,0:T(8,128)}), f32[2,48,3072]{2,1,0:T(8,128)}) %reduce-scatter.49.cloned.1.call-update) | async-done | bytes 1179664 | tf_op jit(solution)/shard_map/reduce_scatter | solution.py:336
  2916.0 6.3 reduce-scatter.47.cloned.1.call-done
  2925.1 20.6 all-reduce.15.cloned.1.call-done
  2960.7 8.5 reduce-scatter.51.cloned.1.call-done
  (487 shorter events, 202.6 us)
Async XLA Ops:
  7.2 54.8 %copy-start.111 = (bf16[2,48]{1,0:T(2,128)(2,1)S(1)}, bf16[2,48]{1,0:T(2,128)(2,1)}, u32[]{:S(2)}) copy-start(bf16[2,48]{1,0:T(2,128)(2,1)} %param.34) | copy-start | bytes 580
  7.2 91.2 %copy-start.110 = (bf16[2,192]{1,0:T(2,128)(2,1)S(1)}, bf16[2,192]{1,0:T(2,128)(2,1)}, u32[]{:S(2)}) copy-start(bf16[2,192]{1,0:T(2,128)(2,1)} %param.32) | copy-start | bytes 2308
  7.3 129.2 %copy-start.106 = (bf16[2,3,48]{2,0,1:T(2,128)(2,1)S(1)}, bf16[2,3,48]{2,0,1:T(2,128)(2,1)}, u32[]{:S(2)}) copy-start(bf16[2,3,48]{2,0,1:T(2,128)(2,1)} %param.25) | copy-start | bytes 1732
  7.3 129.3 %copy-start.107 = (bf16[2,3,48]{2,0,1:T(2,128)(2,1)S(1)}, bf16[2,3,48]{2,0,1:T(2,128)(2,1)}, u32[]{:S(2)}) copy-start(bf16[2,3,48]{2,0,1:T(2,128)(2,1)} %param.26) | copy-start | bytes 1732
  7.3 129.4 %copy-start.108 = (bf16[2,3,48]{2,0,1:T(2,128)(2,1)S(1)}, bf16[2,3,48]{2,0,1:T(2,128)(2,1)}, u32[]{:S(2)}) copy-start(bf16[2,3,48]{2,0,1:T(2,128)(2,1)} %param.27) | copy-start | bytes 1732
  7.3 129.6 %copy-start.109 = (bf16[2,3,48]{2,0,1:T(2,128)(2,1)S(1)}, bf16[2,3,48]{2,0,1:T(2,128)(2,1)}, u32[]{:S(2)}) copy-start(bf16[2,3,48]{2,0,1:T(2,128)(2,1)} %param.30) | copy-start | bytes 1732
  7.3 312.0 %all-gather.12.cloned.1.call-start = ((), (), s32[]{:S(2)}) async-start(), calls=%async_computation.18 | async-start | bytes 7520256 | tf_op jit(solution)/shard_map/all_gather | solution.py:164
  9.2 327.0 %all-gather.14.cloned.1.call-start = ((), (), s32[]{:S(2)}) async-start(), calls=%async_computation.19 | async-start | bytes 2506752 | tf_op jit(solution)/shard_map/all_gather | solution.py:165
  9.9 289.7 %copy-start.47 = (bf16[2,128,768]{2,1,0:T(8,128)(2,1)S(1)}, bf16[2,128,768]{2,1,0:T(8,128)(2,1)}, u32[]{:S(2)}) copy-start(bf16[2,128,768]{2,1,0:T(8,128)(2,1)} %param.20) | copy-start | bytes 1179652
  9.9 289.7 %copy-start.48 = (bf16[2,128,768]{2,1,0:T(8,128)(2,1)S(1)}, bf16[2,128,768]{2,1,0:T(8,128)(2,1)}, u32[]{:S(2)}) copy-start(bf16[2,128,768]{2,1,0:T(8,128)(2,1)} %param.19) | copy-start | bytes 1179652
  10.0 330.7 %all-gather.16.cloned.1.call-start = ((), (), s32[]{:S(2)}) async-start(), calls=%async_computation.20 | async-start | bytes 7520256 | tf_op jit(solution)/shard_map/all_gather | solution.py:169
  11.9 349.6 %all-gather.18.cloned.1.call-start = ((), (), s32[]{:S(2)}) async-start(), calls=%async_computation.21 | async-start | bytes 2506752 | tf_op jit(solution)/shard_map/all_gather | solution.py:170
  12.5 469.7 %all-gather.20.cloned.1.call-start = ((), (), s32[]{:S(2)}) async-start(), calls=%async_computation.22 | async-start | bytes 10027008 | tf_op jit(solution)/shard_map/all_gather | solution.py:174
  13.1 592.3 %all-gather.22.cloned.1.call-start = ((), (), s32[]{:S(2)}) async-start(), calls=%async_computation.23 | async-start | bytes 10027008 | tf_op jit(solution)/shard_map/all_gather | solution.py:176
  13.6 655.0 %all-gather.24.cloned.1.call-start = ((), (), s32[]{:S(2)}) async-start(), calls=%async_computation.24 | async-start | bytes 2506752 | tf_op jit(solution)/shard_map/all_gather | solution.py:178
  14.4 816.4 %reduce-scatter.57.cloned.1.call-start = ((), (), s32[]{:S(2)}) async-start(), calls=%async_computation.35 | async-start | bytes 5013504 | tf_op jit(solution)/shard_map/reduce_scatter | solution.py:340
  299.8 22.3 copy-start.18
  319.2 20.3 copy-start.78
  365.3 240.1 %copy-start = (f32[2,2,128,768]{3,2,1,0:T(8,128)}, f32[2,2,128,768]{3,2,1,0:T(8,128)S(1)}, u32[]{:S(2)}) copy-start(f32[2,2,128,768]{3,2,1,0:T(8,128)S(1)} %get-tuple-element.160) | copy-start | bytes 4718596
  365.3 337.5 %copy-start.59 = (f32[2,2,128]{2,1,0:T(2,128)}, f32[2,2,128]{2,1,0:T(2,128)S(1)}, u32[]{:S(2)}) copy-start(f32[2,2,128]{2,1,0:T(2,128)S(1)} %broadcast_multiply_fusion.1) | copy-start | bytes 6148
  365.6 337.2 %copy-start.63 = (f32[2,2,128]{2,1,0:T(2,128)}, f32[2,2,128]{2,1,0:T(2,128)S(1)}, u32[]{:S(2)}) copy-start(f32[2,2,128]{2,1,0:T(2,128)S(1)} %fusion.99) | copy-start | bytes 6148
  482.2 123.2 %copy-start.57 = (f32[3072,2]{0,1:T(2,128)S(1)}, f32[3072,2]{0,1:T(2,128)}, u32[]{:S(2)}) copy-start(f32[3072,2]{0,1:T(2,128)} %reshape.312) | copy-start | bytes 73732
  482.2 123.2 %copy-start.102 = (f32[768,2]{0,1:T(2,128)S(1)}, f32[768,2]{0,1:T(2,128)}, u32[]{:S(2)}) copy-start(f32[768,2]{0,1:T(2,128)} %reshape.313) | copy-start | bytes 18436
  614.1 54.6 %copy-start.104 = (f32[768]{0:T(1024)S(1)}, f32[768]{0:T(1024)}, u32[]{:S(2)}) copy-start(f32[768]{0:T(1024)} %convert_element_type.421) | copy-start | bytes 9220
  614.1 54.6 %copy-start.114 = (bf16[2,128,768]{2,1,0:T(8,128)(2,1)S(1)}, bf16[2,128,768]{2,1,0:T(8,128)(2,1)}, u32[]{:S(2)}) copy-start(bf16[2,128,768]{2,1,0:T(8,128)(2,1)} %param.37) | copy-start | bytes 1179652
  676.3 279.0 %reduce-scatter.39.cloned.1.call-start = ((), (), s32[]{:S(2)}) async-start(), calls=%async_computation.26 | async-start | bytes 5013504 | tf_op jit(solution)/shard_map/reduce_scatter | solution.py:329
  682.2 11.9 copy-start.37
  731.0 365.9 %reduce-scatter.45.cloned.1.call-start = ((), (), s32[]{:S(2)}) async-start(), calls=%async_computation.29 | async-start | bytes 5013504 | tf_op jit(solution)/shard_map/reduce_scatter | solution.py:334
  735.3 588.8 %reduce-scatter.37.cloned.1.call-start = ((), (), s32[]{:S(2)}) async-start(), calls=%async_computation.25 | async-start | bytes 15040512 | tf_op jit(solution)/shard_map/reduce_scatter | solution.py:328
  771.5 779.2 %reduce-scatter.43.cloned.1.call-start = ((), (), s32[]{:S(2)}) async-start(), calls=%async_computation.28 | async-start | bytes 15040512 | tf_op jit(solution)/shard_map/reduce_scatter | solution.py:333
  794.2 1049.2 %reduce-scatter.53.cloned.1.call-start = ((), (), s32[]{:S(2)}) async-start(), calls=%async_computation.33 | async-start | bytes 20054016 | tf_op jit(solution)/shard_map/reduce_scatter | solution.py:338
  808.0 1161.4 %reduce-scatter.71.cloned.1.call-start = ((), (), s32[]{:S(2)}) async-start(), calls=%async_computation.42 | async-start | bytes 417792
  809.8 1284.9 %reduce-scatter.67.cloned.1.call-start = ((), (), s32[]{:S(2)}) async-start(), calls=%async_computation.40 | async-start | bytes 417792
  812.0 1408.7 %reduce-scatter.65.cloned.1.call-start = ((), (), s32[]{:S(2)}) async-start(), calls=%async_computation.39 | async-start | bytes 417792
  814.2 1531.8 %reduce-scatter.63.cloned.1.call-start = ((), (), s32[]{:S(2)}) async-start(), calls=%async_computation.38 | async-start | bytes 417792
  816.5 1655.4 %reduce-scatter.61.cloned.1.call-start = ((), (), s32[]{:S(2)}) async-start(), calls=%async_computation.37 | async-start | bytes 417792
  818.7 1781.7 %reduce-scatter.69.cloned.1.call-start = ((), (), s32[]{:S(2)}) async-start(), calls=%async_computation.41 | async-start | bytes 1671168
  820.5 2069.8 %reduce-scatter.49.cloned.1.call-start = ((), (), s32[]{:S(2)}) async-start(), calls=%async_computation.31 | async-start | bytes 20054016 | tf_op jit(solution)/shard_map/reduce_scatter | solution.py:336
  830.8 2079.5 %reduce-scatter.59.cloned.1.call-start = ((), (), s32[]{:S(2)}) async-start(), calls=%async_computation.36 | async-start | bytes 221184 | tf_op jit(solution)/shard_map/reduce_scatter | solution.py:381
  832.5 720.2 %copy-start.116 = (u32[32]{0:T(128)S(1)}, u32[32]{0:T(128)}, u32[]{:S(2)}) copy-start(u32[32]{0:T(128)} %constant.49) | copy-start | bytes 388
  832.5 721.5 %copy-start.103 = (f32[768]{0:T(1024)S(1)}, f32[768]{0:T(1024)}, u32[]{:S(2)}) copy-start(f32[768]{0:T(1024)} %get-tuple-element.120) | copy-start | bytes 9220
  832.5 763.7 %copy-start.40 = (bf16[2,2,12,64,128]{4,3,2,1,0:T(8,128)(2,1)S(1)}, bf16[2,2,12,64,128]{4,3,2,1,0:T(8,128)(2,1)}, u32[]{:S(2)}) copy-start(bf16[2,2,12,64,128]{4,3,2,1,0:T(8,128)(2,1)} %copy-done.39) | copy-start | bytes 2359300
  832.5 2080.6 %reduce-scatter.41.cloned.1.call-start = ((), (), s32[]{:S(2)}) async-start(), calls=%async_computation.27 | async-start | bytes 221184 | tf_op jit(solution)/shard_map/reduce_scatter | solution.py:348
  957.0 1965.3 %reduce-scatter.47.cloned.1.call-start = ((), (), s32[]{:S(2)}) async-start(), calls=%async_computation.30 | async-start | bytes 221184 | tf_op jit(solution)/shard_map/reduce_scatter | solution.py:363
  1098.6 1847.1 %all-reduce.15.cloned.1.call-start = ((), (), s32[]{:S(2)}) async-start(), calls=%async_computation.43 | async-start | bytes 1769472
  1552.7 1404.5 %reduce-scatter.55.cloned.1.call-start = ((), (), s32[]{:S(2)}) async-start(), calls=%async_computation.34 | async-start | bytes 884736 | tf_op jit(solution)/shard_map/reduce_scatter | solution.py:375
  1600.0 245.6 %copy-start.21 = (bf16[2,2,12,64,128]{4,3,2,1,0:T(8,128)(2,1)S(1)}, bf16[2,2,12,64,128]{4,3,2,1,0:T(8,128)(2,1)}, u32[]{:S(2)}) copy-start(bf16[2,2,12,64,128]{4,3,2,1,0:T(8,128)(2,1)} %copy-done.20) | copy-start | bytes 2359300
  1845.6 1123.6 %reduce-scatter.51.cloned.1.call-start = ((), (), s32[]{:S(2)}) async-start(), calls=%async_computation.32 | async-start | bytes 884736 | tf_op jit(solution)/shard_map/reduce_scatter | solution.py:369
  (99 other events, 331.8 us)
Sparse Core Ops, SparseCore 0:
  11.4 105.1 all-gather.11
  119.3 63.8 all-gather.13
  186.4 108.2 all-gather.15
  297.2 61.1 all-gather.17
  361.0 121.2 all-gather.19
  484.8 120.5 all-gather.21
  608.1 60.5 all-gather.23
  676.4 136.1 reduce-scatter.56
  818.6 136.6 reduce-scatter.38
  960.3 136.5 reduce-scatter.44
  1103.7 220.3 reduce-scatter.36
  1329.7 220.9 reduce-scatter.42
  1557.4 285.9 reduce-scatter.52
  1848.6 120.7 reduce-scatter.70
  1973.9 120.7 reduce-scatter.66
  2099.9 120.7 reduce-scatter.64
  2225.2 120.6 reduce-scatter.62
  2351.1 120.7 reduce-scatter.60
  2476.7 123.6 reduce-scatter.68
  2606.0 284.1 reduce-scatter.48
  2893.0 6.6 reduce-scatter.58
  2902.6 8.6 reduce-scatter.40
  2913.5 8.7 reduce-scatter.46
  2925.1 20.5 all-reduce.14
  2948.0 9.2 reduce-scatter.54
  2960.0 9.1 reduce-scatter.50
where the time goes:
time: 2990 us; the launch traced here: 2980 us
  waiting for transfers between devices  2310 us (77%)
  blocking collectives  351 us (12%)
  matrix products  163 us (5%)
  local copies, waits for them, and re-layouts  76.8 us (3%)
  other arithmetic  59.5 us (2%)
    unnamed x33, waiting for transfers between devices  767 us
    reduce_scatter x1, waiting for transfers between devices, on_device(): lax.psum_scatter(grad_ffn_in, 'dp', scatter_dimension=1, tiled=True)  284 us
    reduce_scatter x1, waiting for transfers between devices, on_device(): lax.psum_scatter(grad_ffn_out, 'dp', scatter_dimension=1, tiled=True)  243 us
    reduce_scatter x1, waiting for transfers between devices, on_device(): lax.psum_scatter(grad_cross_weights, 'dp', scatter_dimension=2, tiled=True)  225 us
    reduce_scatter x1, waiting for transfers between devices, on_device(): lax.psum_scatter(grad_self_weights, 'dp', scatter_dimension=2, tiled=True)  225 us
    reduce_scatter x1, waiting for transfers between devices, on_device(): lax.psum_scatter(grad_self_projection, 'dp', scatter_dimension=1, tiled=T...  140 us
    reduce_scatter x1, waiting for transfers between devices, on_device(): lax.psum_scatter(grad_cross_projection, 'dp', scatter_dimension=1, tiled=...  123 us
    all_gather x1, waiting for transfers between devices, on_device(): lax.all_gather(ffn_in, 'dp', axis=1, tiled=True)  117 us
  transfers between devices with their start and end apart: 26, of which 19 were waited for; matrix products, arithmetic and copies ran while one was open for 9% of the time, Pallas kernels for 0%

commit v1 on v0

v1 whole, which is shorter than its diff:
```python
import functools

import jax
import jax.numpy as jnp
from jax import lax
from jax.experimental import pallas as pl
from jax.experimental.pallas import tpu as pltpu
from jax.sharding import PartitionSpec as P

HEADS = 12
HEAD = 64
norm_epsilon = 1e-05
bf16 = jnp.bfloat16
f32 = jnp.float32
AXES = ("dp", "rep")
TILE = 256
VMEM_LIMIT = 56 << 20
ANY = pl.BlockSpec(memory_space=pl.ANY)
VMEM = pl.BlockSpec(memory_space=pltpu.VMEM)
SMEM = pl.BlockSpec(memory_space=pltpu.SMEM)


class Grid:
    def __init__(self, mesh):
        self.n = mesh.shape["dp"]
        self.r = mesh.shape["rep"]
        self.high = self.n >> 1
        self.partner = self.n >> 2
        self.groups = [0, self.partner, self.high, self.high | self.partner]
        low = []
        bit = 1
        while bit < self.partner:
            low.append(bit)
            bit *= 2
        self.orders = [low, low[::-1]]

    def across(self, values, mask):
        pairs = [
            (d * self.r + c, (d ^ mask) * self.r + c) for d in range(self.n) for c in range(self.r)
        ]
        return lax.ppermute(values, AXES, pairs)

    def swap_cores(self, values):
        pairs = [
            (d * self.r + c, d * self.r + (c ^ 1)) for d in range(self.n) for c in range(self.r)
        ]
        return lax.ppermute(values, AXES, pairs)

    def piece_masks(self, stream):
        masks = [0]
        for bit in self.orders[stream]:
            masks = masks + [m ^ bit for m in masks]
        return masks


def call(kernel, outs, ins, specs, out_specs, scratch=(), flops=0, moved=0):
    return pl.pallas_call(
        kernel,
        out_shape=[jax.ShapeDtypeStruct(shape, dtype) for shape, dtype in outs],
        in_specs=specs,
        out_specs=out_specs,
        scratch_shapes=list(scratch),
        compiler_params=pltpu.CompilerParams(vmem_limit_bytes=VMEM_LIMIT),
        cost_estimate=pl.CostEstimate(flops=flops, bytes_accessed=moved, transcendentals=0),
    )(*ins)


def regroup_kernel(*refs):
    sources, outs = refs[:4], refs[4:]
    for k, source in enumerate(sources):
        for j, out in enumerate(outs):
            out[k] = source[j]


def regroup(sources):
    shape = sources[0].shape
    if shape[1] % 16:
        stacked = jnp.stack(sources, 1)
        return [stacked[0], stacked[1]]
    return call(
        regroup_kernel,
        [((4,) + shape[1:], bf16)] * 2,
        sources,
        [VMEM] * 4,
        [VMEM] * 2,
        moved=16 * shape[1] * shape[2] * 2,
    )


def place_kernel(grid, info_ref, *refs):
    sources, out_ref, sem = refs[:-2], refs[-2], refs[-1]
    count = len(sources) // 2
    me = info_ref[2]
    for j in range(2):
        masks = grid.piece_masks(j)
        for q in range(count):
            for g, group in enumerate(grid.groups):
                target = jnp.bitwise_xor(me, masks[q] ^ group)
                pltpu.make_async_copy(
                    sources[j * count + q].at[g], out_ref.at[j, target], sem
                ).start()
    pltpu.make_async_copy(out_ref, out_ref, sem).wait()


def place(grid, info, pieces):
    rows, width = pieces[0][0].shape[1:]
    if rows % 16:
        result = []
        for j in range(2):
            masks = [m ^ g for m in grid.piece_masks(j) for g in grid.groups]
            at = [masks.index(i) for i in range(grid.n)]
            order = jnp.take(jnp.array(at), jnp.arange(grid.n) ^ info[2])
            result.append(jnp.take(jnp.concatenate(pieces[j], 0), order, axis=0))
        return jnp.stack(result)
    sources = pieces[0] + pieces[1]
    return call(
        functools.partial(place_kernel, grid),
        [((2, grid.n, rows, width), bf16)],
        [info] + sources,
        [SMEM] + [ANY] * len(sources),
        [VMEM],
        [pltpu.SemaphoreType.DMA],
        moved=4 * grid.n * rows * width * 2,
    )[0]


def gather_round(grid, info, mine, theirs):
    bufs = regroup(
        [
            mine,
            grid.across(theirs, grid.groups[1]),
            grid.across(theirs, grid.groups[2]),
            grid.across(mine, grid.groups[3]),
        ]
    )
    pieces = []
    for j in range(2):
        held = [bufs[j]]
        for bit in grid.orders[j]:
            held = held + [grid.across(piece, bit) for piece in held]
            if len(grid.orders[j]) > 2:
                held = [jnp.concatenate(held, 0)]
        if len(grid.orders[j]) > 2:
            held = [held[0][4 * q : 4 * q + 4] for q in range(grid.n // 4)]
        pieces.append(held)
    own = place(grid, info, pieces)
    return own, grid.swap_cores(own)


def split_kernel(grid, info_ref, keep, received, *outs):
    count = len(outs) // 2
    me = info_ref[2]
    for j in range(2):
        masks = grid.piece_masks(j)
        for q in range(count):
            for g, group in enumerate(grid.groups):
                source = jnp.bitwise_xor(me, masks[q] ^ group)
                total = keep[j, source].astype(f32) + received[j, source].astype(f32)
                outs[j * count + q][g] = total.astype(bf16)


def split(grid, info, keep, received):
    n, rows, width = keep.shape[1:]
    count = n // 4
    if rows % 16:
        total = (keep.astype(f32) + received.astype(f32)).astype(bf16)
        pieces = []
        for j in range(2):
            masks = jnp.array([m ^ g for m in grid.piece_masks(j) for g in grid.groups])
            by_slot = jnp.take(total[j], masks ^ info[2], axis=0)
            pieces.append([by_slot[4 * q : 4 * q + 4] for q in range(count)])
        return pieces
    outs = call(
        functools.partial(split_kernel, grid),
        [((4, rows, width), bf16)] * (2 * count),
        [info, keep, received],
        [SMEM, VMEM, VMEM],
        [VMEM] * (2 * count),
        moved=6 * n * rows * width * 2,
    )
    return [outs[:count], outs[count:]]


def added(a, b):
    return (a.astype(f32) + b.astype(f32)).astype(bf16)


def scatter_round(grid, info, keep, send):
    pieces = split(grid, info, keep, grid.swap_cores(send))
    owned = []
    for j in range(2):
        held = pieces[j]
        for bit in reversed(grid.orders[j]):
            half = len(held) // 2
            if len(grid.orders[j]) > 2:
                received = grid.across(jnp.concatenate(held[half:], 0), bit)
                received = [received[4 * q : 4 * q + 4] for q in range(half)]
            else:
                received = [grid.across(piece, bit) for piece in held[half:]]
            held = [added(a, b) for a, b in zip(held[:half], received, strict=True)]
        owned.append(held[0])
    stacked = jnp.stack(owned)
    near = stacked[:, 0].astype(f32) + grid.across(stacked[:, 3], grid.groups[3]).astype(f32)
    far = grid.across(stacked[:, 1], grid.groups[1]).astype(f32) + grid.across(
        stacked[:, 2], grid.groups[2]
    ).astype(f32)
    return near, far


def nn(a, b):
    return lax.dot_general(a, b, (((1,), (0,)), ((), ())), preferred_element_type=f32)


def nt(a, b):
    return lax.dot_general(a, b, (((1,), (1,)), ((), ())), preferred_element_type=f32)


def tn(a, b):
    return lax.dot_general(a, b, (((0,), (0,)), ((), ())), preferred_element_type=f32)


def tiles(extent, body, size=TILE):
    def step(i, carry):
        body(pl.ds(pl.multiple_of(i * size, size), size))
        return carry

    lax.fori_loop(0, extent // size, step, 0)


def load_blocks(core, own, swapped, blocks, sem):
    count = own.shape[0]
    copies = []
    for j in range(count):
        copies.append(pltpu.make_async_copy(own.at[j], blocks.at[core * count + j], sem.at[j]))
        copies.append(
            pltpu.make_async_copy(
                swapped.at[j], blocks.at[(1 - core) * count + j], sem.at[count + j]
            )
        )
    for copy in copies:
        copy.start()

    def wait():
        for copy in copies:
            copy.wait()

    return wait


def store_blocks(core, blocks, keep, send, sem):
    count = keep.shape[0]
    copies = []
    for j in range(count):
        copies.append(pltpu.make_async_copy(blocks.at[core * count + j], keep.at[j], sem.at[j]))
        copies.append(
            pltpu.make_async_copy(
                blocks.at[(1 - core) * count + j], send.at[j], sem.at[count + j]
            )
        )
    for copy in copies:
        copy.start()
    for copy in copies:
        copy.wait()


def normalised(values):
    mean_row = jnp.mean(values, axis=-1, keepdims=True)
    centred = values - mean_row
    variance = jnp.mean(centred * centred, axis=-1, keepdims=True)
    scale = lax.rsqrt(variance + norm_epsilon)
    return centred * scale, scale


def norm_back(values, grads, gain):
    unit, scale = normalised(values)
    scaled = grads * gain
    first = jnp.mean(scaled, axis=-1, keepdims=True)
    second = jnp.mean(scaled * unit, axis=-1, keepdims=True)
    return (scaled - first - unit * second) * scale, grads * unit


def lane_masks():
    lanes = lax.broadcasted_iota(jnp.int32, (128, 2 * HEAD), 1)
    left = (lanes < HEAD).astype(f32).astype(bf16)
    right = (lanes >= HEAD).astype(f32).astype(bf16)
    return lanes < HEAD, left, right


def two_heads(values, left, right):
    return jnp.concatenate([values * left, values * right], 0)


def softened(queries, keys_both, count):
    scores = nt(queries, keys_both) * HEAD ** (-0.5)
    slots = queries.shape[0]
    valid = lax.broadcasted_iota(jnp.int32, (slots, slots), 1) < count
    halves = []
    for half in (scores[:, :slots], scores[:, slots:]):
        half = jnp.where(valid, half, -1000000000.0)
        weights = jnp.exp(half - jnp.max(half, axis=-1, keepdims=True))
        halves.append(weights / jnp.sum(weights, axis=-1, keepdims=True))
    return jnp.concatenate(halves, 1)


def attend_kernel(
    cross,
    slots,
    info_ref,
    counts_ref,
    vec_ref,
    *refs,
):
    if cross:
        lang, vis, lang_far, vis_far, own_w, swapped_w = refs[:6]
        refs = refs[6:]
    else:
        residual_ref, low_ref, own_w, swapped_w = refs[:4]
        refs = refs[4:]
    q_ref, k_ref, v_ref, o_ref, sum_ref, norm_ref, norm_low_ref = refs[:7]
    blocks, sem = refs[7:9]
    core = info_ref[1]
    rows = q_ref.shape[0]
    half = rows // 2
    wait_blocks = load_blocks(core, own_w, swapped_w, blocks, sem)
    if cross:
        src_ref, oth_ref, in_sem = refs[9:12]

        def copies(mine, mine_far, other, other_far):
            return [
                pltpu.make_async_copy(mine, src_ref.at[pl.ds(0, half)], in_sem.at[0]),
                pltpu.make_async_copy(mine_far, src_ref.at[pl.ds(half, half)], in_sem.at[1]),
                pltpu.make_async_copy(other, oth_ref.at[pl.ds(0, half)], in_sem.at[2]),
                pltpu.make_async_copy(other_far, oth_ref.at[pl.ds(half, half)], in_sem.at[3]),
            ]

        @pl.when(info_ref[0] == 0)
        def _():
            for copy in copies(lang, lang_far, vis, vis_far):
                copy.start()

        @pl.when(info_ref[0] != 0)
        def _():
            for copy in copies(vis, vis_far, lang, lang_far):
                copy.start()

        for copy in copies(lang, lang_far, vis, vis_far):
            copy.wait()
    else:
        src_ref = oth_ref = low_ref
    wait_blocks()
    width = q_ref.shape[1]

    def project_tile(at):
        q_ref[:, at] = (nn(src_ref[...], blocks[0, :, at]) + vec_ref[0:1, at]).astype(bf16)
        k_ref[:, at] = nn(oth_ref[...], blocks[1, :, at]).astype(bf16)
        v_ref[:, at] = (nn(oth_ref[...], blocks[2, :, at]) + vec_ref[1:2, at]).astype(bf16)

    tiles(width, project_tile)
    unused, left, right = lane_masks()

    def one_page(page, carry):
        at_rows = pl.ds(pl.multiple_of(page * slots, slots), slots)
        count = counts_ref[page]
        for pair in range(width // 128):
            lanes = slice(pair * 128, pair * 128 + 128)
            soft = softened(
                q_ref[at_rows, lanes], two_heads(k_ref[at_rows, lanes], left, right), count
            ).astype(bf16)
            mixed = nn(soft, two_heads(v_ref[at_rows, lanes], left, right))
            o_ref[at_rows, lanes] = mixed.astype(bf16)
        return carry

    lax.fori_loop(0, rows // slots, one_page, 0)

    def out_tile(at):
        out = nn(o_ref[...], blocks[3, :, at]) + vec_ref[2:3, at]
        if cross:
            sum_ref[:, at] = src_ref[:, at].astype(f32) + out
        else:
            sum_ref[:, at] = residual_ref[:, at] + out

    tiles(width, out_tile)

    def norm_rows(at):
        result = normalised(sum_ref[at, :])[0] * vec_ref[3:4, :] + vec_ref[4:5, :]
        norm_ref[at, :] = result
        norm_low_ref[at, :] = result.astype(bf16)

    tiles(rows, norm_rows, 128)


def attend(cross, slots, info, counts, vectors, inputs, weights):
    width = weights[0].shape[-1]
    rows = counts.shape[0] * slots
    blocks = (4, width, width)
    scratch = [pltpu.VMEM(blocks, bf16), pltpu.SemaphoreType.DMA((4,))]
    if cross:
        scratch += [pltpu.VMEM((rows, width), bf16)] * 2 + [pltpu.SemaphoreType.DMA((4,))]
    return call(
        functools.partial(attend_kernel, cross, slots),
        [((rows, width), bf16)] * 4 + [((rows, width), f32)] * 2 + [((rows, width), bf16)],
        [info, counts, vectors] + list(inputs) + list(weights),
        [SMEM, SMEM, VMEM] + ([ANY] * 4 if cross else [VMEM] * 2) + [ANY] * 2,
        [VMEM] * 7,
        scratch,
        flops=8 * rows * width * width + 8 * rows * slots * width,
        moved=4 * width * width * 2 + rows * width * 20,
    )


def hidden_kernel(info_ref, shift_ref, low_ref, own_w, swapped_w, active_ref, slope_ref, blocks, sem):
    wait_blocks = load_blocks(info_ref[1], own_w, swapped_w, blocks, sem)
    wait_blocks()
    width = low_ref.shape[1]
    for b in range(4):

        def tile(at, b=b):
            wide = pl.ds(pl.multiple_of(at.start + b * width, TILE), TILE)
            hidden = nn(low_ref[...], blocks[b, :, at]) + shift_ref[0:1, wide]
            square = hidden * hidden
            bent = jnp.tanh(0.7978845608028654 * (hidden + 0.044715 * square * hidden))
            active_ref[:, wide] = (0.5 * hidden * (1.0 + bent)).astype(bf16)
            slope = 0.5 * (1.0 + bent) + 0.5 * hidden * (1.0 - bent * bent) * (
                0.7978845608028654 * (1.0 + 3.0 * 0.044715 * square)
            )
            slope_ref[:, wide] = slope.astype(bf16)

        tiles(width, tile)


def hidden_layer(info, shift, low, weights):
    rows, width = low.shape
    return call(
        hidden_kernel,
        [((rows, 4 * width), bf16)] * 2,
        [info, shift, low] + list(weights),
        [SMEM, VMEM, VMEM, ANY, ANY],
        [VMEM, VMEM],
        [pltpu.VMEM((4, width, width), bf16), pltpu.SemaphoreType.DMA((4,))],
        flops=8 * rows * width * width,
        moved=8 * width * width + rows * width * 18,
    )


def load_wide(core, own, swapped, wide, sem):
    n, rows = own.shape[1:3]
    for j in range(2):
        for which, source in ((core, own), (1 - core, swapped)):

            def body(p, carry, j=j, which=which, source=source):
                at = pl.multiple_of((4 * p + 2 * which + j) * rows, 16)
                pltpu.make_async_copy(source.at[j, p], wide.at[pl.ds(at, rows)], sem).start()
                return carry

            lax.fori_loop(0, n, body, 0)


def store_wide(core, wide, keep, send, sem):
    n, rows = keep.shape[1:3]
    for j in range(2):
        for which, target in ((core, keep), (1 - core, send)):

            def body(p, carry, j=j, which=which, target=target):
                at = pl.multiple_of((4 * p + 2 * which + j) * rows, 16)
                pltpu.make_async_copy(wide.at[pl.ds(at, rows)], target.at[j, p], sem).start()
                return carry

            lax.fori_loop(0, n, body, 0)
    pltpu.make_async_copy(wide, wide, sem).wait()


def branch_kernel(
    wide_in,
    info_ref,
    vec_ref,
    active_ref,
    residual_ref,
    *refs,
):
    if wide_in:
        own_w, swapped_w, sum_ref, norm_ref, far_ref, wide, sem = refs
        load_wide(info_ref[1], own_w, swapped_w, wide, sem)
        pltpu.make_async_copy(wide, wide, sem).wait()
    else:
        whole_w, sum_ref, norm_ref, far_ref, wide, sem = refs
        copy = pltpu.make_async_copy(whole_w, wide, sem)
        copy.start()
        copy.wait()
    rows, width = residual_ref.shape
    half = rows // 2

    def tile(at):
        out = nn(active_ref[...], wide[:, at]) + vec_ref[0:1, at]
        sum_ref[:, at] = residual_ref[:, at] + out

    tiles(width, tile)

    def norm_rows(at):
        result = normalised(sum_ref[at, :])[0] * vec_ref[1:2, :] + vec_ref[2:3, :]
        norm_ref[at, :] = result

    tiles(half, norm_rows, 128)

    def norm_far(at):
        below = pl.ds(pl.multiple_of(at.start + half, 128), 128)
        result = normalised(sum_ref[below, :])[0] * vec_ref[1:2, :] + vec_ref[2:3, :]
        far_ref[at, :] = result.astype(bf16)

    tiles(half, norm_far, 128)


def branch_layer(info, vectors, active, residual, weights):
    rows, width = residual.shape
    wide_in = len(weights) == 2
    return call(
        functools.partial(branch_kernel, wide_in),
        [((rows, width), f32), ((rows // 2, width), f32), ((rows // 2, width), bf16)],
        [info, vectors, active, residual] + list(weights),
        [SMEM, VMEM, VMEM, VMEM] + [ANY] * len(weights),
        [VMEM] * 3,
        [pltpu.VMEM((4 * width, width), bf16), pltpu.SemaphoreType.DMA],
        flops=8 * rows * width * width,
        moved=8 * width * width + rows * width * 20,
    )


def gate_kernel(
    info_ref,
    shift_ref,
    third_ref,
    far_ref,
    cotangent_ref,
    own_w,
    swapped_w,
    united_ref,
    grad_own_ref,
    grad_far_ref,
    grad_shift_ref,
    keep_ref,
    send_ref,
    blocks,
    sem,
    grads,
    mix_ref,
    low_ref,
):
    core = info_ref[1]
    side = info_ref[0]
    load_blocks(core, own_w, swapped_w, blocks, sem)()
    rows, width = third_ref.shape
    part = width // 2
    low_ref[...] = third_ref[...].astype(bf16)
    for h in range(2):
        at = slice(h * part, (h + 1) * part)
        logits = nn(low_ref[...], blocks[h]) + nn(far_ref[...], blocks[2 + h]) + shift_ref[0:1, at]
        mixing = 1.0 / (1.0 + jnp.exp(-logits))
        first = side == 0
        share = jnp.where(first, mixing, 1.0 - mixing)
        mine, other = third_ref[:, at], far_ref[:, at].astype(f32)
        united_ref[:, at] = (share * mine + (1.0 - share) * other).astype(bf16)
        cotangent = cotangent_ref[:, at].astype(f32)
        gap = jnp.where(first, mine - other, other - mine)
        grad = (cotangent * gap * mixing * (1.0 - mixing)).astype(bf16)
        mix_ref[:, at] = grad
        grad_own_ref[:, at] = cotangent * share
        grad_shift_ref[0:1, at] = jnp.sum(grad.astype(f32), axis=0, keepdims=True)
        grads[h] = tn(low_ref[...], grad).astype(bf16)
        grads[2 + h] = tn(far_ref[...], grad).astype(bf16)
    left, right = mix_ref[:, :part], mix_ref[:, part:]
    for t in range(width // TILE):
        at = slice(t * TILE, (t + 1) * TILE)
        cotangent = cotangent_ref[:, at].astype(f32)
        direct = grad_own_ref[:, at]
        back = nt(left, blocks[0, at]) + nt(right, blocks[1, at])
        back_far = nt(left, blocks[2, at]) + nt(right, blocks[3, at])
        grad_own_ref[:, at] = direct + back
        grad_far_ref[:, at] = (cotangent - direct + back_far).astype(bf16)
    store_blocks(core, grads, keep_ref, send_ref, sem)


def gate_layer(info, shift, third, far, cotangent, weights):
    rows, width = third.shape
    blocks = (4, width, width // 2)
    return call(
        gate_kernel,
        [
            ((rows, width), bf16),
            ((rows, width), f32),
            ((rows, width), bf16),
            ((8, width), f32),
            ((2,) + blocks[1:], bf16),
            ((2,) + blocks[1:], bf16),
        ],
        [info, shift, third, far, cotangent] + list(weights),
        [SMEM] + [VMEM] * 4 + [ANY] * 2,
        [VMEM] * 4 + [ANY] * 2,
        [
            pltpu.VMEM(blocks, bf16),
            pltpu.SemaphoreType.DMA((4,)),
            pltpu.VMEM(blocks, bf16),
            pltpu.VMEM((rows, width), bf16),
            pltpu.VMEM((rows, width), bf16),
        ],
        flops=12 * rows * width * width,
        moved=8 * width * width + rows * width * 14,
    )


def branch_back_kernel(
    wide_out,
    info_ref,
    gain_ref,
    sum_ref,
    grad_own_ref,
    grad_far_ref,
    active_ref,
    grad_sum_ref,
    grad_low_ref,
    vec_ref,
    *refs,
):
    rows, width = sum_ref.shape
    half = rows // 2
    vec_ref[...] = jnp.zeros_like(vec_ref)

    def norm_rows(at, offset, grads):
        below = pl.ds(pl.multiple_of(at.start + offset, 128), 128)
        back, gain_rows = norm_back(sum_ref[below, :], grads, gain_ref[0:1, :])
        low = back.astype(bf16)
        grad_sum_ref[below, :] = back
        grad_low_ref[below, :] = low
        vec_ref[0:1, :] += jnp.sum(gain_rows, axis=0, keepdims=True)
        vec_ref[1:2, :] += jnp.sum(grads, axis=0, keepdims=True)
        vec_ref[2:3, :] += jnp.sum(low.astype(f32), axis=0, keepdims=True)

    tiles(half, lambda at: norm_rows(at, 0, grad_own_ref[at, :]), 128)
    tiles(half, lambda at: norm_rows(at, half, grad_far_ref[at, :].astype(f32)), 128)
    wide, sem = refs[-2:]

    def tile(at):
        wide[at, :] = tn(active_ref[:, at], grad_low_ref[...]).astype(bf16)

    tiles(4 * width, tile)
    if wide_out:
        store_wide(info_ref[1], wide, refs[0], refs[1], sem)
    else:
        copy = pltpu.make_async_copy(wide, refs[0], sem)
        copy.start()
        copy.wait()


def branch_back(grid, info, gain, sums, grad_own, grad_far, active, piece):
    rows, width = sums.shape
    wide_out = piece % 16 == 0
    target = (2, grid.n, piece, width) if wide_out else (4 * width, width)
    outs = [(target, bf16)] * (2 if wide_out else 1)
    return call(
        functools.partial(branch_back_kernel, wide_out),
        [((rows, width), f32), ((rows, width), bf16), ((8, width), f32)] + outs,
        [info, gain, sums, grad_own, grad_far, active],
        [SMEM] + [VMEM] * 5,
        [VMEM] * 3 + [ANY] * len(outs),
        [pltpu.VMEM((4 * width, width), bf16), pltpu.SemaphoreType.DMA],
        flops=8 * rows * width * width,
        moved=8 * width * width + rows * width * 24,
    )


def hidden_back_kernel(
    wide_in,
    info_ref,
    grad_low_ref,
    slope_ref,
    low_ref,
    *refs,
):
    core = info_ref[1]
    grad_hidden_ref, vec_ref, keep_ref, send_ref, wide, sem, grads, out_sem = refs[-8:]
    if wide_in:
        load_wide(core, refs[0], refs[1], wide, sem)
        pltpu.make_async_copy(wide, wide, sem).wait()
    else:
        copy = pltpu.make_async_copy(refs[0], wide, sem)
        copy.start()
        copy.wait()
    width = low_ref.shape[1]
    for b in range(4):

        def tile(at, b=b):
            cols = pl.ds(pl.multiple_of(at.start + b * width, TILE), TILE)
            back = nt(grad_low_ref[...], wide[cols, :]) * slope_ref[:, cols].astype(f32)
            low = back.astype(bf16)
            grad_hidden_ref[:, cols] = low
            vec_ref[0:1, cols] = jnp.sum(low.astype(f32), axis=0, keepdims=True)
            grads[b, :, at] = tn(low_ref[...], low).astype(bf16)

        tiles(width, tile)
    store_blocks(core, grads, keep_ref, send_ref, out_sem)


def hidden_back(info, grad_low, slope, low, weights):
    rows, width = low.shape
    blocks = (4, width, width)
    return call(
        functools.partial(hidden_back_kernel, len(weights) == 2),
        [((rows, 4 * width), bf16), ((8, 4 * width), f32)] + [((2,) + blocks[1:], bf16)] * 2,
        [info, grad_low, slope, low] + list(weights),
        [SMEM] + [VMEM] * 3 + [ANY] * len(weights),
        [VMEM] * 2 + [ANY] * 2,
        [
            pltpu.VMEM((4 * width, width), bf16),
            pltpu.SemaphoreType.DMA,
            pltpu.VMEM(blocks, bf16),
            pltpu.SemaphoreType.DMA((4,)),
        ],
        flops=16 * rows * width * width,
        moved=16 * width * width + rows * width * 30,
    )


def second_back_kernel(
    info_ref,
    gain_ref,
    sum_ref,
    grad_ref,
    grad_hidden_ref,
    own_w,
    swapped_w,
    grad_sum_ref,
    vec_ref,
    blocks,
    sem,
):
    load_blocks(info_ref[1], own_w, swapped_w, blocks, sem)()
    rows, width = sum_ref.shape

    def tile(at):
        total = grad_ref[:, at]
        for b in range(4):
            total += nt(grad_hidden_ref[:, b * width : (b + 1) * width], blocks[b, at, :])
        grad_sum_ref[:, at] = total

    tiles(width, tile)
    norm_back_rows(sum_ref, grad_sum_ref, gain_ref, vec_ref, rows)


def norm_back_rows(sum_ref, grad_ref, gain_ref, vec_ref, rows):
    vec_ref[0:2, :] = jnp.zeros_like(vec_ref[0:2, :])

    def norm_rows(at):
        grads = grad_ref[at, :]
        back, gain_rows = norm_back(sum_ref[at, :], grads, gain_ref[0:1, :])
        grad_ref[at, :] = back
        vec_ref[0:1, :] += jnp.sum(gain_rows, axis=0, keepdims=True)
        vec_ref[1:2, :] += jnp.sum(grads, axis=0, keepdims=True)

    tiles(rows, norm_rows, 128)


def second_back(info, gain, sums, grads, grad_hidden, weights):
    rows, width = sums.shape
    return call(
        second_back_kernel,
        [((rows, width), f32), ((8, width), f32)],
        [info, gain, sums, grads, grad_hidden] + list(weights),
        [SMEM] + [VMEM] * 4 + [ANY] * 2,
        [VMEM] * 2,
        [pltpu.VMEM((4, width, width), bf16), pltpu.SemaphoreType.DMA((4,))],
        flops=8 * rows * width * width,
        moved=8 * width * width + rows * width * 20,
    )


def attend_back_kernel(cross, slots, info_ref, counts_ref, gain_ref, grad_ref, *refs):
    q_ref, k_ref, v_ref, o_ref = refs[:4]
    refs = refs[4:]
    if cross:
        lang, vis, lang_far, vis_far, own_w, swapped_w = refs[:6]
        own_ref, own_far_ref, oth_ref_out, oth_far_ref, vec_ref, keep_ref, send_ref = refs[6:13]
        refs = refs[13:]
    else:
        low_ref, sum_ref, own_w, swapped_w = refs[:4]
        out_ref, vec_ref, keep_ref, send_ref = refs[4:8]
        refs = refs[8:]
    blocks, sem, grads, low_grad, grad_o, dq_ref, dk_ref, dv_ref = refs[:8]
    core = info_ref[1]
    rows, width = q_ref.shape
    half = rows // 2
    wait_blocks = load_blocks(core, own_w, swapped_w, blocks, sem)
    if cross:
        src_ref, oth_ref, in_sem = refs[8:11]

        def copies(mine, mine_far, other, other_far):
            return [
                pltpu.make_async_copy(mine, src_ref.at[pl.ds(0, half)], in_sem.at[0]),
                pltpu.make_async_copy(mine_far, src_ref.at[pl.ds(half, half)], in_sem.at[1]),
                pltpu.make_async_copy(other, oth_ref.at[pl.ds(0, half)], in_sem.at[2]),
                pltpu.make_async_copy(other_far, oth_ref.at[pl.ds(half, half)], in_sem.at[3]),
            ]

        @pl.when(info_ref[0] == 0)
        def _():
            for copy in copies(lang, lang_far, vis, vis_far):
                copy.start()

        @pl.when(info_ref[0] != 0)
        def _():
            for copy in copies(vis, vis_far, lang, lang_far):
                copy.start()

    else:
        src_ref = oth_ref = low_ref
    vec_ref[...] = jnp.zeros_like(vec_ref)

    def lower(at):
        low = grad_ref[at, :].astype(bf16)
        low_grad[at, :] = low
        vec_ref[4:5, :] += jnp.sum(low.astype(f32), axis=0, keepdims=True)

    tiles(rows, lower, 128)
    wait_blocks()

    def project_tile(at):
        grad_o[:, at] = nt(low_grad[...], blocks[3, at, :]).astype(bf16)
        grads[3, at, :] = tn(o_ref[:, at], low_grad[...]).astype(bf16)

    tiles(width, project_tile)
    left_lanes, left, right = lane_masks()

    def one_page(page, carry):
        at_rows = pl.ds(pl.multiple_of(page * slots, slots), slots)
        count = counts_ref[page]
        for pair in range(width // 128):
            lanes = slice(pair * 128, pair * 128 + 128)
            queries = q_ref[at_rows, lanes]
            keys = two_heads(k_ref[at_rows, lanes], left, right)
            values = two_heads(v_ref[at_rows, lanes], left, right)
            grad_pair = grad_o[at_rows, lanes]
            soft = softened(queries, keys, count)
            grad_soft = nt(grad_pair, values)
            dv = tn(soft.astype(bf16), grad_pair)
            dv_ref[at_rows, lanes] = jnp.where(left_lanes, dv[:slots], dv[slots:]).astype(bf16)
            weighted = soft * grad_soft
            parts = []
            for h in range(2):
                cut = slice(h * slots, (h + 1) * slots)
                row_sum = jnp.sum(weighted[:, cut], axis=-1, keepdims=True)
                parts.append(weighted[:, cut] - soft[:, cut] * row_sum)
            grad_scores = jnp.concatenate(parts, 1).astype(bf16)
            dq = nn(grad_scores, keys) * HEAD ** (-0.5)
            dq_ref[at_rows, lanes] = dq.astype(bf16)
            dk = tn(grad_scores, queries) * HEAD ** (-0.5)
            dk_ref[at_rows, lanes] = jnp.where(left_lanes, dk[:slots], dk[slots:]).astype(bf16)
        return carry

    lax.fori_loop(0, rows // slots, one_page, 0)

    def sum_rows(at):
        vec_ref[2:3, :] += jnp.sum(dq_ref[at, :].astype(f32), axis=0, keepdims=True)
        vec_ref[3:4, :] += jnp.sum(dv_ref[at, :].astype(f32), axis=0, keepdims=True)

    tiles(rows, sum_rows, 128)
    if cross:
        for copy in copies(lang, lang_far, vis, vis_far):
            copy.wait()

    def weight_tile(at):
        grads[0, at, :] = tn(src_ref[:, at], dq_ref[...]).astype(bf16)
        grads[1, at, :] = tn(oth_ref[:, at], dk_ref[...]).astype(bf16)
        grads[2, at, :] = tn(oth_ref[:, at], dv_ref[...]).astype(bf16)

    tiles(width, weight_tile)

    def input_tile(at):
        mine = grad_ref[:, at] + nt(dq_ref[...], blocks[0, at, :])
        other = nt(dk_ref[...], blocks[1, at, :]) + nt(dv_ref[...], blocks[2, at, :])
        if cross:
            own_ref[:, at] = mine[:half]
            own_far_ref[:, at] = mine[half:].astype(bf16)
            oth_ref_out[:, at] = other[:half]
            oth_far_ref[:, at] = other[half:].astype(bf16)
        else:
            out_ref[:, at] = mine + other

    tiles(width, input_tile)
    if not cross:
        norm_back_rows(sum_ref, out_ref, gain_ref, vec_ref, rows)
    store_blocks(core, grads, keep_ref, send_ref, sem)


def attend_back(cross, slots, info, counts, gain, grad, saved, inputs, weights):
    rows, width = grad.shape
    blocks = (4, width, width)
    whole = pltpu.VMEM((rows, width), bf16)
    scratch = [
        pltpu.VMEM(blocks, bf16),
        pltpu.SemaphoreType.DMA((4,)),
        pltpu.VMEM(blocks, bf16),
    ] + [whole] * 5
    half = (rows // 2, width)
    if cross:
        scratch += [whole, whole, pltpu.SemaphoreType.DMA((4,))]
        outs = [(half, f32), (half, bf16), (half, f32), (half, bf16)]
    else:
        outs = [((rows, width), f32)]
    return call(
        functools.partial(attend_back_kernel, cross, slots),
        outs + [((8, width), f32)] + [((2,) + blocks[1:], bf16)] * 2,
        [info, counts, gain, grad] + list(saved) + list(inputs) + list(weights),
        [SMEM, SMEM] + [VMEM] * 6 + ([ANY] * 4 if cross else [VMEM] * 2) + [ANY] * 2,
        [VMEM] * (len(outs) + 1) + [ANY] * 2,
        scratch,
        flops=16 * rows * width * width + 24 * rows * slots * width,
        moved=16 * width * width + rows * width * 26,
    )


def reorder(values, hits):
    hits = hits.reshape(hits.shape + (1,) * (values.ndim - 1))
    return jnp.sum(jnp.where(hits, values.astype(f32)[None], 0.0), axis=1)


def on_device(
    grid,
    language_in,
    vision_in,
    language_count,
    vision_count,
    cross_qkv,
    cross_proj,
    cross_bias,
    norm_gain,
    norm_bias,
    self_qkv,
    self_proj,
    self_bias,
    ffn_in,
    ffn_in_bias,
    ffn_out,
    ffn_out_bias,
    gate_weight,
    gate_bias,
    cotangent,
):
    n = grid.n
    me = lax.axis_index("dp")
    core = lax.axis_index("rep")
    side = ((me // grid.high) ^ (me // grid.partner)) & 1
    first = side == 0
    info = jnp.stack([side, core, me]).astype(jnp.int32)
    rows, width = cross_proj.shape[1:]
    dim = n * rows
    pages, slots = language_in.shape[:2]
    wide_ok = rows % 16 == 0

    def own(pair):
        return lax.dynamic_index_in_dim(pair, side, 0, keepdims=False)

    def other(pair):
        return lax.dynamic_index_in_dim(pair, 1 - side, 0, keepdims=False)

    def gathered(blocks):
        stacked = jnp.stack(blocks, 1)
        stacked = stacked.reshape((2, 2, 2) + stacked.shape[2:])
        stacked = lax.dynamic_index_in_dim(stacked, core, 1, keepdims=False)
        return gather_round(grid, info, own(stacked), other(stacked))

    def natural(pair):
        return [w.reshape(2, dim, w.shape[-1]) for w in pair]

    cross_w = natural(gathered([cross_qkv[:, 0], cross_qkv[:, 1], cross_qkv[:, 2], cross_proj]))
    language = language_in.reshape(pages * slots, width)
    vision = vision_in.reshape(pages * slots, width)
    language_far = grid.across(language, grid.partner)
    vision_far = grid.across(vision, grid.partner)
    counts_mine = jnp.stack([language_count, vision_count])
    counts_far = grid.across(counts_mine, grid.partner)
    counts = jnp.concatenate([own(counts_mine), own(counts_far)])
    other_counts = jnp.concatenate([other(counts_mine), other(counts_far)])

    vectors = jnp.concatenate(
        [
            cross_bias,
            self_bias,
            norm_gain,
            norm_bias,
            ffn_in_bias.reshape(2, 4, rows),
            ffn_out_bias[:, None],
            jnp.broadcast_to(gate_bias[None, None], (2, 1, rows)),
        ],
        1,
    ).reshape(2, 18 * rows)
    pad = -(18 * rows) % 1024
    vectors = jnp.pad(vectors, ((0, 0), (0, pad))).reshape(2, 1, -1, 128)
    vec_mine, vec_theirs = own(vectors), other(vectors)
    held = jnp.concatenate(
        [
            vec_mine,
            grid.across(vec_theirs, grid.groups[1]),
            grid.across(vec_theirs, grid.groups[2]),
            grid.across(vec_mine, grid.groups[3]),
        ],
        0,
    )
    for bit in grid.orders[0]:
        held = jnp.concatenate([held, grid.across(held, bit)], 0)
    masks = jnp.array([m ^ g for m in grid.piece_masks(0) for g in grid.groups], jnp.int32)
    hits = (masks ^ me)[None, :] == jnp.arange(n)[:, None]
    vec_full = reorder(held, hits).reshape(n, -1)[:, : 18 * rows].reshape(n, 18, rows)
    vec_rows = vec_full.transpose(1, 0, 2).reshape(18, dim)
    ffn_in_shift = vec_full[:, 12:16].reshape(1, 4 * dim)

    def rows_of(*indices):
        return jnp.stack([vec_rows[i] for i in indices])

    self_w = natural(gathered([self_qkv[:, 0], self_qkv[:, 1], self_qkv[:, 2], self_proj]))
    in_w = natural(gathered([ffn_in[:, :, i * width : (i + 1) * width] for i in range(4)]))
    out_w = gathered([ffn_out[:, i * rows : (i + 1) * rows] for i in range(4)])
    if not wide_ok:
        both = jnp.where(core == 0, jnp.stack(out_w), jnp.stack(out_w[::-1]))
        out_w = [both.reshape(4, n, rows, width).transpose(1, 0, 2, 3).reshape(4 * dim, width)]
    part = width // 2
    turned = gate_weight[::-1]
    gate_w = natural(
        gathered(
            [gate_weight[:, :, :part], gate_weight[:, :, part:], turned[:, :, :part], turned[:, :, part:]]
        )
    )

    inputs = [language, vision, language_far, vision_far]
    cq, ck, cv, co, first_sum, first_norm, first_low = attend(
        True, slots, info, other_counts, rows_of(0, 1, 2, 6, 9), inputs, cross_w
    )
    sq, sk, sv, so, second_sum, second_norm, second_low = attend(
        False, slots, info, counts, rows_of(3, 4, 5, 7, 10), [first_norm, first_low], self_w
    )
    active, slope = hidden_layer(info, ffn_in_shift, second_low, in_w)
    third_sum, third_own, third_send = branch_layer(
        info, rows_of(16, 8, 11), active, second_norm, out_w
    )
    third_far = grid.across(third_send, grid.partner)
    united, grad_third_own, grad_third_send, grad_gate_shift, gate_keep, gate_send = gate_layer(
        info, rows_of(17), third_own, third_far, cotangent.reshape(pages * slots, width), gate_w
    )
    grad_third_far = grid.across(grad_third_send, grid.partner)

    def by_piece(pair):
        return [g.reshape(2, n, rows, g.shape[-1]) for g in pair]

    gate_done = scatter_round(grid, info, *by_piece([gate_keep, gate_send]))
    grad_third_sum, grad_branch_low, vec_third, *out_grads = branch_back(
        grid, info, rows_of(8), third_sum, grad_third_own, grad_third_far, active, rows
    )
    if not wide_ok:
        by_core = out_grads[0].reshape(n, 2, 2, rows, width).transpose(1, 2, 0, 3, 4)
        out_grads = [
            lax.dynamic_index_in_dim(by_core, c, 0, keepdims=False) for c in (core, 1 - core)
        ]
    out_done = scatter_round(grid, info, *out_grads)
    grad_hidden, vec_hidden, in_keep, in_send = hidden_back(
        info, grad_branch_low, slope, second_low, out_w
    )
    in_done = scatter_round(grid, info, *by_piece([in_keep, in_send]))
    grad_second_sum, vec_second = second_back(
        info, rows_of(7), second_sum, grad_third_sum, grad_hidden, in_w
    )
    grad_first_sum, vec_self, self_keep, self_send = attend_back(
        False,
        slots,
        info,
        counts,
        rows_of(6),
        grad_second_sum,
        [sq, sk, sv, so],
        [first_low, first_sum],
        self_w,
    )
    self_done = scatter_round(grid, info, *by_piece([self_keep, self_send]))
    grad_own, grad_own_far, grad_oth, grad_oth_far, vec_cross, cross_keep, cross_send = attend_back(
        True,
        slots,
        info,
        other_counts,
        rows_of(6),
        grad_first_sum,
        [cq, ck, cv, co],
        inputs,
        cross_w,
    )
    grad_mine = grad_own + grid.across(grad_oth_far, grid.partner).astype(f32)
    grad_theirs = grad_oth + grid.across(grad_own_far, grid.partner).astype(f32)
    cross_done = scatter_round(grid, info, *by_piece([cross_keep, cross_send]))
    page_shape = language_in.shape
    grad_language = jnp.where(first, grad_mine, grad_theirs).astype(bf16).reshape(page_shape)
    grad_vision = jnp.where(first, grad_theirs, grad_mine).astype(bf16).reshape(page_shape)

    grad_rows = jnp.stack(
        [vec_cross[2], vec_cross[3], vec_cross[4]]
        + [vec_self[2], vec_self[3], vec_self[4]]
        + [vec_self[0], vec_second[0], vec_third[0]]
        + [vec_self[1], vec_second[1], vec_third[1]]
    ).reshape(12, n, rows)
    grad_tail = jnp.stack([vec_third[2], grad_gate_shift[0]]).reshape(2, n, rows)
    grad_vec = jnp.concatenate(
        [
            grad_rows.transpose(1, 0, 2),
            vec_hidden[0].reshape(n, 4, rows),
            grad_tail.transpose(1, 0, 2),
        ],
        1,
    ).reshape(n, 18 * rows)
    grad_vec = jnp.pad(grad_vec, ((0, 0), (0, pad))).reshape(n, -1, 128)
    grad_vec = reorder(grad_vec, hits.T)
    grad_vec = grad_vec + grid.swap_cores(grad_vec)
    for bit in reversed(grid.orders[0]):
        half = grad_vec.shape[0] // 2
        grad_vec = grad_vec[:half] + grid.across(grad_vec[half:], bit)
    vec_near = grad_vec[0] + grid.across(grad_vec[3], grid.groups[3])
    vec_far = grid.across(grad_vec[1], grid.groups[1]) + grid.across(grad_vec[2], grid.groups[2])
    vec_near = vec_near.reshape(-1)[: 18 * rows].reshape(18, rows)
    vec_far = vec_far.reshape(-1)[: 18 * rows].reshape(18, rows)

    def sides(near, far):
        return jnp.where(first, jnp.stack([near, far]), jnp.stack([far, near]))

    vec_both = sides(vec_near, vec_far)

    def finished(done):
        mine = jnp.stack(done).astype(bf16)
        far = grid.swap_cores(mine)
        whole = jnp.where(core == 0, jnp.stack([mine, far], 1), jnp.stack([far, mine], 1))
        return whole.reshape((2, 4) + whole.shape[3:]).astype(f32)

    def by_side(done):
        whole = finished(done)
        return jnp.where(first, whole, whole[::-1])

    cross_all = by_side(cross_done)
    self_all = by_side(self_done)
    in_all = by_side(in_done)
    out_all = by_side(out_done)
    gate_all = finished(gate_done)
    gate_near = gate_all[0, :2] + gate_all[1, 2:]
    gate_far = gate_all[0, 2:] + gate_all[1, :2]
    gate_both = sides(
        jnp.concatenate([gate_near[0], gate_near[1]], -1),
        jnp.concatenate([gate_far[0], gate_far[1]], -1),
    )
    return (
        united.reshape(page_shape),
        grad_language,
        grad_vision,
        cross_all[:, 0:3],
        cross_all[:, 3],
        vec_both[:, 0:3],
        vec_both[:, 6:9],
        vec_both[:, 9:12],
        self_all[:, 0:3],
        self_all[:, 3],
        vec_both[:, 3:6],
        in_all.transpose(0, 2, 1, 3).reshape(2, rows, 4 * width),
        vec_both[:, 12:16].reshape(2, 4 * rows),
        out_all.reshape(2, 4 * rows, width),
        vec_both[:, 16],
        gate_both,
        vec_near[17] + vec_far[17],
    )


def solution(mesh):
    whole = P(("dp", "rep"), None, None)
    weights = (
        P(None, None, "dp", None),
        P(None, "dp", None),
        P(None, None, "dp"),
        P(None, None, "dp"),
        P(None, None, "dp"),
        P(None, None, "dp", None),
        P(None, "dp", None),
        P(None, None, "dp"),
        P(None, "dp", None),
        P(None, "dp"),
        P(None, "dp", None),
        P(None, "dp"),
        P(None, "dp", None),
        P("dp"),
    )
    return jax.shard_map(
        functools.partial(on_device, Grid(mesh)),
        mesh=mesh,
        in_specs=(whole, whole, P(("dp", "rep")), P(("dp", "rep"))) + weights + (whole,),
        out_specs=(whole, whole, whole) + weights,
        check_vma=False,
    )
```

time: 2990 us -> 608 us (0.20)
  waiting for transfers between devices: 2310 us -> 199 us
  blocking collectives: 351 us -> 0 us
  Pallas kernels: 0 us -> 209 us
  matrix products: 163 us -> 0 us
  starting transfers between devices: 1.53 us -> 139 us
  local copies, waits for them, and re-layouts: 76.8 us -> 32.3 us
  other arithmetic: 59.5 us -> 16.2 us
    reduce_scatter x12 -> x0, waiting for transfers between devices: 1260 us -> none  [the longest x1 284 us: on_device(): lax.psum_scatter(grad_ffn_in, 'dp', scatter_dimension=1, tiled=True)]
    unnamed x33 -> x0, waiting for transfers between devices: 767 us -> none
    all_gather x7 -> x0, waiting for transfers between devices: 285 us -> none  [the longest x1 117 us: on_device(): lax.all_gather(ffn_in, 'dp', axis=1, tiled=True)]
    all_gather x19 -> x0, blocking collectives: 262 us -> none  [the longest x1 42.8 us: on_device(): lax.all_gather(cross_bias, 'dp', axis=2, tiled=True)]
    pallas_call x0 -> x25, Pallas kernels: none -> 209 us  [call(): pl.pallas_call(kernel, out_shape=[jax.ShapeDtypeStruct(shape, dtype) for...]
    ppermute x0 -> x123, waiting for transfers between devices: none -> 199 us  [the longest x107 198 us: across(): return lax.ppermute(values, AXES, pairs)]
    dot_general x45 -> x0, matrix products: 163 us -> none  [the longest x10 47.2 us: weight_grad(): jnp.einsum('spnd,spne->sde', values, grads_low, preferred_element_type=jn...]
    ppermute x0 -> x123, starting transfers between devices: none -> 139 us  [the longest x107 137 us: across(): return lax.ppermute(values, AXES, pairs)]
  transfers between devices with their start and end apart: 26 -> 123, of which waited for: 19 -> 49; matrix products, arithmetic and copies ran while one was open for 9% -> 6% of each run, Pallas kernels for 0% -> 34%
where the time goes in v1:
time: 608 us; the launch traced here: 598 us
  Pallas kernels  209 us (34%)
  waiting for transfers between devices  199 us (33%)
  starting transfers between devices  139 us (23%)
  local copies, waits for them, and re-layouts  32.3 us (5%)
  other arithmetic  16.2 us (3%)
    pallas_call x25, Pallas kernels, call(): pl.pallas_call(kernel, out_shape=[jax.ShapeDtypeStruct(shape, dtype) for...  209 us
    ppermute x107, waiting for transfers between devices, across(): return lax.ppermute(values, AXES, pairs)  198 us
    ppermute x107, starting transfers between devices, across(): return lax.ppermute(values, AXES, pairs)  137 us
  transfers between devices with their start and end apart: 123, of which 49 were waited for; matrix products, arithmetic and copies ran while one was open for 6% of the time, Pallas kernels for 34%

profile of v1, /device:TPU:0, one launch (start us, length us, event | category | flops | bytes accessed | tf_op | source)
XLA Modules:
  0.0 598.2 jit_solution(5602839467191366751)
XLA Ops:
  5.9 4.1 collective-permute-start.1
  13.2 3.9 collective-permute-start.2
  27.3 3.8 collective-permute-start.51
  40.2 7.2 %collective-permute-start.28 = (bf16[2,48,768]{2,1,0:T(8,128)(2,1)S(1)}, bf16[2,48,768]{2,1,0:T(8,128)(2,1)S(1)}, u32[]{:S(2)}, u32[]{:S(2)}) collective-permute-start(bf16[2,48,768]{2,1,0:T(8,128)(2,1)S(1)} %get-tuple-element.317), channel_id=1, source_target_pairs={{0,8},{1,9},{2,10},{3,11},{4,12},{5,13},{6,14},{7,15},{8,0},{9,1},... | collective-permute-start | bytes 442376 | tf_op jit(solution)/shard_map/ppermute | solution.py:41
  47.4 8.5 %collective-permute-done.19.refs_2_ = bf16[2,48,768]{2,1,0:T(8,128)(2,1)S(1)} collective-permute-done((bf16[2,48,768]{2,1,0:T(8,128)(2,1)S(1)}, bf16[2,48,768]{2,1,0:T(8,128)(2,1)S(1)}, u32[]{:S(2)}, u32[]{:S(2)}) %collective-permute-start.19) | collective-permute-done | bytes 147488 | tf_op jit(solution)/shard_map/ppermute | solution.py:41
  61.6 5.5 collective-permute-done.29.refs_2_
  88.2 4.8 collective-permute-done.22.refs_2_
  100.9 4.8 collective-permute-done.32.refs_2_
  113.5 4.8 collective-permute-done.13.refs_3_
  121.0 3.9 shard_map.324
  129.9 3.9 shard_map.327
  139.5 3.8 shard_map.330
  150.0 3.7 shard_map.333.refs_0_
  155.5 4.6 collective-permute-done.55.refs_5_
  161.7 3.8 collective-permute-done.54.refs_3_
  166.0 4.7 collective-permute-done.57.refs_7_
  172.1 7.7 %collective-permute-done.6.refs_2_.refs_6_ = bf16[256,768]{1,0:T(8,128)(2,1)S(1)} collective-permute-done((bf16[256,768]{1,0:T(8,128)(2,1)S(1)}, bf16[256,768]{1,0:T(8,128)(2,1)S(1)}, u32[]{:S(2)}, u32[]{:S(2)}) %collective-permute-start.6) | collective-permute-done | bytes 393248 | tf_op jit(solution)/shard_map/ppermute | solution.py:41
  188.2 14.9 %shard_map.325 = (bf16[512,768]{1,0:T(8,128)(2,1)}, bf16[512,768]{1,0:T(8,128)(2,1)}, bf16[512,768]{1,0:T(8,128)(2,1)}, bf16[512,768]{1,0:T(8,128)(2,1)}, f32[51...) custom-call(s32[3]{0:T(128)} %pad_add_fusion.1.info_ref, s32[4]{0:T(128)} %pad_add_fusion.3.counts_ref, ...), custom_call_target="tpu_custom_call" | custom-call | flops 2818572288 | bytes 12582912 | tf_op jit(solution)/shard_map/pallas_call | solution.py:57
  203.1 15.2 %shard_map.328 = (bf16[512,768]{1,0:T(8,128)(2,1)}, bf16[512,768]{1,0:T(8,128)(2,1)}, bf16[512,768]{1,0:T(8,128)(2,1)}, bf16[512,768]{1,0:T(8,128)(2,1)}, f32[51...) custom-call(s32[3]{0:T(128)} %pad_add_fusion.1.info_ref, s32[4]{0:T(128)} %pad_add_fusion.2.counts_ref, ...), custom_call_target="tpu_custom_call" | custom-call | flops 2818572288 | bytes 12582912 | tf_op jit(solution)/shard_map/pallas_call | solution.py:57
  219.7 13.7 %shard_map.331 = (bf16[512,3072]{1,0:T(8,128)(2,1)}, bf16[512,3072]{1,0:T(8,128)(2,1)}) custom-call(s32[3]{0:T(128)} %pad_add_fusion.1.info_ref, f32[1,3072]{1,0:T(1,128)} %reshape.509.shift_ref, bf16[512,768]{1,0:T(8,128)(2,1)} %get-tuple-element.120.low_ref, bf16[2,768,768]{2,1,0:T(8,128)(2,1)} %bitcast.308, bf16[2,768,768]{2,1,0:T(8,128)(2,1)} %bitcast.314), custom_call_target="tpu_custom_call" | custom-call | flops 2415919104 | bytes 11796480 | tf_op jit(solution)/shard_map/pallas_call | solution.py:57
  233.4 10.1 %shard_map.334 = (f32[512,768]{1,0:T(8,128)}, f32[256,768]{1,0:T(8,128)}, bf16[256,768]{1,0:T(8,128)(2,1)}) custom-call(s32[3]{0:T(128)} %pad_add_fusion.1.info_ref, f32[3,768]{1,0:T(4,128)} %pad_maximum_fusion.16.vec_ref, bf16[512,3072]{1,0:T(8,128)(2,1)} %get-tuple-element.123.active_ref, f32[512,768]{1,0:T(8,128)} %get-tuple-element.124.residual_ref, ...), custom_call_target="tpu_custom_call" | custom-call | flops 2415919104 | bytes 12582912 | tf_op jit(solution)/shard_map/pallas_call | solution.py:57
  245.5 9.8 %collective-permute-done.48.far_ref = bf16[256,768]{1,0:T(8,128)(2,1)S(1)} collective-permute-done((bf16[256,768]{1,0:T(8,128)(2,1)}, bf16[256,768]{1,0:T(8,128)(2,1)S(1)}, u32[]{:S(2)}, u32[]{:S(2)}) %collective-permute-start.48) | collective-permute-done | bytes 393248 | tf_op jit(solution)/shard_map/ppermute | solution.py:41
  256.0 8.1 %shard_map.337 = (bf16[256,768]{1,0:T(8,128)(2,1)}, f32[256,768]{1,0:T(8,128)}, bf16[256,768]{1,0:T(8,128)(2,1)}, f32[8,768]{1,0:T(8,128)}, bf16[2,768,384]{2,1,0:T(8,128)(2,1)}, /*index=5*/bf16[2,768,384]{2,1,0:T(8,128)(2,1)}) custom-call(s32[3]{0:T(128)} %pad_add_fusion.1.info_ref, f32[1,768]{1,0:T(1,128)} %slice.339.shift_ref, ...), custom_call_target="tpu_custom_call" | custom-call | flops 1811939328 | bytes 7471104 | tf_op jit(solution)/shard_map/pallas_call | solution.py:57
  266.2 9.0 %collective-permute-done.59.grad_far_ref = bf16[256,768]{1,0:T(8,128)(2,1)S(1)} collective-permute-done((bf16[256,768]{1,0:T(8,128)(2,1)}, bf16[256,768]{1,0:T(8,128)(2,1)S(1)}, u32[]{:S(2)}, u32[]{:S(2)}) %collective-permute-start.59) | collective-permute-done | bytes 393248 | tf_op jit(solution)/shard_map/ppermute | solution.py:41
  275.9 13.1 %shard_map.338 = (f32[512,768]{1,0:T(8,128)}, bf16[512,768]{1,0:T(8,128)(2,1)}, f32[8,768]{1,0:T(8,128)}, bf16[2,16,48,768]{3,2,1,0:T(8,128)(2,1)}, bf16[2,16,48,768]{3,2,1,0:T(8,128)(2,1)}) custom-call(s32[3]{0:T(128)} %pad_add_fusion.1.info_ref, f32[1,768]{1,0:T(1,128)} %copy-done.83, f32[512,768]{1,0:T(8,128)} %get-tuple-element.133.sum_ref, ...), custom_call_target="tpu_custom_call" | custom-call | flops 2415919104 | bytes 14155776 | tf_op jit(solution)/shard_map/pallas_call | solution.py:57
  289.0 21.3 %shard_map.339 = (bf16[512,3072]{1,0:T(8,128)(2,1)}, f32[8,3072]{1,0:T(8,128)}, bf16[2,768,768]{2,1,0:T(8,128)(2,1)}, bf16[2,768,768]{2,1,0:T(8,128)(2,1)}) custom-call(s32[3]{0:T(128)} %pad_add_fusion.1.info_ref, bf16[512,768]{1,0:T(8,128)(2,1)} %get-tuple-element.137.grad_low_ref, bf16[512,3072]{1,0:T(8,128)(2,1)} %get-tuple-element.138.slope_ref, ...), custom_call_target="tpu_custom_call" | custom-call | flops 4831838208 | bytes 21233664 | tf_op jit(solution)/shard_map/pallas_call | solution.py:57
  310.3 10.8 %shard_map.340 = (f32[512,768]{1,0:T(8,128)}, f32[8,768]{1,0:T(8,128)}) custom-call(s32[3]{0:T(128)} %pad_add_fusion.1.info_ref, f32[1,768]{1,0:T(1,128)} %copy-done.81, f32[512,768]{1,0:T(8,128)} %get-tuple-element.132.sum_ref, f32[512,768]{1,0:T(8,128)} %get-tuple-element.136.grad_ref, bf16[512,3072]{1,0:T(8,128)(2,1)} %get-tuple-element.139.grad_hidden_ref, ...), custom_call_target="tpu_custom_call" | custom-call | flops 2415919104 | bytes 12582912 | tf_op jit(solution)/shard_map/pallas_call | solution.py:57
  321.2 28.1 %shard_map.341 = (f32[512,768]{1,0:T(8,128)}, f32[8,768]{1,0:T(8,128)}, bf16[2,768,768]{2,1,0:T(8,128)(2,1)}, bf16[2,768,768]{2,1,0:T(8,128)(2,1)}) custom-call(s32[3]{0:T(128)} %pad_add_fusion.1.info_ref, s32[4]{0:T(128)} %pad_add_fusion.2.counts_ref, f32[1,768]{1,0:T(1,128)} %copy-done.82, f32[512,768]{1,0:T(8,128)} %get-tuple-element.140.grad_ref, ...), custom_call_target="tpu_custom_call" | custom-call | flops 6039797760 | bytes 19660800 | tf_op jit(solution)/shard_map/pallas_call | solution.py:57
  352.6 25.9 %shard_map.342 = (f32[256,768]{1,0:T(8,128)}, bf16[256,768]{1,0:T(8,128)(2,1)}, f32[256,768]{1,0:T(8,128)}, bf16[256,768]{1,0:T(8,128)(2,1)}, f32[8,768]{1,0:T(8...) custom-call(s32[3]{0:T(128)} %pad_add_fusion.1.info_ref, s32[4]{0:T(128)} %pad_add_fusion.3.counts_ref, ...), custom_call_target="tpu_custom_call" | custom-call | flops 6039797760 | bytes 19660800 | tf_op jit(solution)/shard_map/pallas_call | solution.py:57
  386.8 3.4 collective-permute-done.75
  409.4 4.6 collective-permute-done.117
  431.1 4.2 collective-permute-start.121
  446.1 5.6 collective-permute-done.61
  453.9 4.3 shard_map.343
  462.1 4.3 shard_map.344
  468.1 4.3 shard_map.345
  473.3 4.4 shard_map.346
  479.7 7.8 %collective-permute-done.81 = bf16[4,48,768]{2,1,0:T(8,128)(2,1)S(1)} collective-permute-done((bf16[4,48,768]{2,1,0:T(8,128)(2,1)S(1)}, bf16[4,48,768]{2,1,0:T(8,128)(2,1)S(1)}, u32[]{:S(2)}, u32[]{:S(2)}) %collective-permute-start.81) | collective-permute-done | bytes 294944 | tf_op jit(solution)/shard_map/ppermute | solution.py:41
  489.4 5.8 collective-permute-done.92
  497.1 5.0 collective-permute-done.103
  506.1 6.0 collective-permute-done.65
  516.5 8.2 %collective-permute-done.82 = bf16[4,48,768]{2,1,0:T(8,128)(2,1)S(1)} collective-permute-done((bf16[4,48,768]{2,1,0:T(8,128)(2,1)S(1)}, bf16[4,48,768]{2,1,0:T(8,128)(2,1)S(1)}, u32[]{:S(2)}, u32[]{:S(2)}) %collective-permute-start.82) | collective-permute-done | bytes 294944 | tf_op jit(solution)/shard_map/ppermute | solution.py:41
  529.2 8.1 %collective-permute-done.93 = bf16[4,48,768]{2,1,0:T(8,128)(2,1)S(1)} collective-permute-done((bf16[4,48,768]{2,1,0:T(8,128)(2,1)S(1)}, bf16[4,48,768]{2,1,0:T(8,128)(2,1)S(1)}, u32[]{:S(2)}, u32[]{:S(2)}) %collective-permute-start.93) | collective-permute-done | bytes 294944 | tf_op jit(solution)/shard_map/ppermute | solution.py:41
  542.4 5.4 collective-permute-done.104
  554.0 5.0 collective-permute-done.70
  559.2 9.8 %collective-permute-done.88 = bf16[2,48,768]{2,1,0:T(8,128)(2,1)S(1)} collective-permute-done((bf16[2,48,768]{2,1,0:T(8,128)(2,1)S(1)}, bf16[2,48,768]{2,1,0:T(8,128)(2,1)S(1)}, u32[]{:S(2)}, u32[]{:S(2)}) %collective-permute-start.88) | collective-permute-done | bytes 147488 | tf_op jit(solution)/shard_map/ppermute | solution.py:41
  571.3 8.8 %collective-permute-done.99 = bf16[2,48,768]{2,1,0:T(8,128)(2,1)S(1)} collective-permute-done((bf16[2,48,768]{2,1,0:T(8,128)(2,1)S(1)}, bf16[2,48,768]{2,1,0:T(8,128)(2,1)S(1)}, u32[]{:S(2)}, u32[]{:S(2)}) %collective-permute-start.99) | collective-permute-done | bytes 147488 | tf_op jit(solution)/shard_map/ppermute | solution.py:41
  585.5 4.7 collective-permute-done.110
  (605 shorter events, 222.4 us)
Async XLA Ops:
  12.6 18.4 %collective-permute-start.50 = (bf16[2,48,384]{2,1,0:T(8,128)(2,1)S(1)}, bf16[2,48,384]{2,1,0:T(8,128)(2,1)S(1)}, u32[]{:S(2)}, u32[]{:S(2)}) collective-permute-start(bf16[2,48,384]{2,1,0:T(8,128)(2,1)S(1)} %get-tuple-element.338), channel_id=1, source_target_pairs={{0,16},{1,17},{2,18},{3,19},{4,20},{5,21},{6,22},{7,23},{8,24},{9,... | collective-permute-start | bytes 221192 | tf_op jit(solution)/shard_map/ppermute | solution.py:41
  13.1 18.1 %collective-permute-start.49 = (bf16[2,48,384]{2,1,0:T(8,128)(2,1)S(1)}, bf16[2,48,384]{2,1,0:T(8,128)(2,1)S(1)}, u32[]{:S(2)}, u32[]{:S(2)}) collective-permute-start(bf16[2,48,384]{2,1,0:T(8,128)(2,1)S(1)} %get-tuple-element.338), channel_id=1, source_target_pairs={{0,8},{1,9},{2,10},{3,11},{4,12},{5,13},{6,14},{7,15},{8,0},{9,1},... | collective-permute-start | bytes 221192 | tf_op jit(solution)/shard_map/ppermute | solution.py:41
  19.2 18.8 %collective-permute-start.9 = (bf16[2,48,768]{2,1,0:T(8,128)(2,1)S(1)}, bf16[2,48,768]{2,1,0:T(8,128)(2,1)S(1)}, u32[]{:S(2)}, u32[]{:S(2)}) collective-permute-start(bf16[2,48,768]{2,1,0:T(8,128)(2,1)S(1)} %get-tuple-element.325), channel_id=1, source_target_pairs={{0,16},{1,17},{2,18},{3,19},{4,20},{5,21},{6,22},{7,23},{8,24},{9,... | collective-permute-start | bytes 442376 | tf_op jit(solution)/shard_map/ppermute | solution.py:41
  25.3 14.8 %collective-permute-start.8 = (bf16[2,48,768]{2,1,0:T(8,128)(2,1)S(1)}, bf16[2,48,768]{2,1,0:T(8,128)(2,1)S(1)}, u32[]{:S(2)}, u32[]{:S(2)}) collective-permute-start(bf16[2,48,768]{2,1,0:T(8,128)(2,1)S(1)} %get-tuple-element.325), channel_id=1, source_target_pairs={{0,8},{1,9},{2,10},{3,11},{4,12},{5,13},{6,14},{7,15},{8,0},{9,1},... | collective-permute-start | bytes 442376 | tf_op jit(solution)/shard_map/ppermute | solution.py:41
  31.2 24.8 %collective-permute-start.19 = (bf16[2,48,768]{2,1,0:T(8,128)(2,1)S(1)}, bf16[2,48,768]{2,1,0:T(8,128)(2,1)S(1)}, u32[]{:S(2)}, u32[]{:S(2)}) collective-permute-start(bf16[2,48,768]{2,1,0:T(8,128)(2,1)S(1)} %get-tuple-element.323), channel_id=1, source_target_pairs={{0,16},{1,17},{2,18},{3,19},{4,20},{5,21},{6,22},{7,23},{8,24},{9,... | collective-permute-start | bytes 442376 | tf_op jit(solution)/shard_map/ppermute | solution.py:41
  34.9 22.9 %collective-permute-start.18 = (bf16[2,48,768]{2,1,0:T(8,128)(2,1)S(1)}, bf16[2,48,768]{2,1,0:T(8,128)(2,1)S(1)}, u32[]{:S(2)}, u32[]{:S(2)}) collective-permute-start(bf16[2,48,768]{2,1,0:T(8,128)(2,1)S(1)} %get-tuple-element.323), channel_id=1, source_target_pairs={{0,8},{1,9},{2,10},{3,11},{4,12},{5,13},{6,14},{7,15},{8,0},{9,1},... | collective-permute-start | bytes 442376 | tf_op jit(solution)/shard_map/ppermute | solution.py:41
  38.0 21.9 %collective-permute-start.20 = (bf16[2,48,768]{2,1,0:T(8,128)(2,1)S(1)}, bf16[2,48,768]{2,1,0:T(8,128)(2,1)S(1)}, u32[]{:S(2)}, u32[]{:S(2)}) collective-permute-start(bf16[2,48,768]{2,1,0:T(8,128)(2,1)S(1)} %get-tuple-element.324.refs_0_), channel_id=1, source_target_pairs={{0,24},{1,25},{2,26},{3,27},{4,28},{5,29},{6,30},{7,31},{8,16},{9,... | collective-permute-start | bytes 442376 | tf_op jit(solution)/shard_map/ppermute | solution.py:41
  40.1 27.0 %collective-permute-start.29 = (bf16[2,48,768]{2,1,0:T(8,128)(2,1)S(1)}, bf16[2,48,768]{2,1,0:T(8,128)(2,1)S(1)}, u32[]{:S(2)}, u32[]{:S(2)}) collective-permute-start(bf16[2,48,768]{2,1,0:T(8,128)(2,1)S(1)} %get-tuple-element.317), channel_id=1, source_target_pairs={{0,16},{1,17},{2,18},{3,19},{4,20},{5,21},{6,22},{7,23},{8,24},{9,... | collective-permute-start | bytes 442376 | tf_op jit(solution)/shard_map/ppermute | solution.py:41
  40.2 26.9 %collective-permute-start.28 = (bf16[2,48,768]{2,1,0:T(8,128)(2,1)S(1)}, bf16[2,48,768]{2,1,0:T(8,128)(2,1)S(1)}, u32[]{:S(2)}, u32[]{:S(2)}) collective-permute-start(bf16[2,48,768]{2,1,0:T(8,128)(2,1)S(1)} %get-tuple-element.317), channel_id=1, source_target_pairs={{0,8},{1,9},{2,10},{3,11},{4,12},{5,13},{6,14},{7,15},{8,0},{9,1},... | collective-permute-start | bytes 442376 | tf_op jit(solution)/shard_map/ppermute | solution.py:41
  57.8 14.3 %collective-permute-start.39 = (bf16[2,48,768]{2,1,0:T(8,128)(2,1)S(1)}, bf16[2,48,768]{2,1,0:T(8,128)(2,1)S(1)}, u32[]{:S(2)}, u32[]{:S(2)}) collective-permute-start(bf16[2,48,768]{2,1,0:T(8,128)(2,1)S(1)} %get-tuple-element.311), channel_id=1, source_target_pairs={{0,16},{1,17},{2,18},{3,19},{4,20},{5,21},{6,22},{7,23},{8,24},{9,... | collective-permute-start | bytes 442376 | tf_op jit(solution)/shard_map/ppermute | solution.py:41
  59.9 20.9 %collective-permute-start.12 = (bf16[4,48,768]{2,1,0:T(8,128)(2,1)}, bf16[4,48,768]{2,1,0:T(8,128)(2,1)S(1)}, u32[]{:S(2)}, u32[]{:S(2)}) collective-permute-start(bf16[4,48,768]{2,1,0:T(8,128)(2,1)} %get-tuple-element.114.refs_0_), channel_id=1, source_target_pairs={{0,4},{1,5},{2,6},{3,7},{4,0},{5,1},{6,2},{7,3},{8,12},{9,13},{10,... | collective-permute-start | bytes 884744 | tf_op jit(solution)/shard_map/ppermute | solution.py:41
  82.0 16.0 %collective-permute-start.25 = (bf16[4,48,768]{2,1,0:T(8,128)(2,1)}, bf16[4,48,768]{2,1,0:T(8,128)(2,1)S(1)}, u32[]{:S(2)}, u32[]{:S(2)}) collective-permute-start(bf16[4,48,768]{2,1,0:T(8,128)(2,1)} %get-tuple-element.119.refs_4_), channel_id=1, source_target_pairs={{0,2},{1,3},{2,0},{3,1},{4,6},{5,7},{6,4},{7,5},{8,10},{9,11},{10,... | collective-permute-start | bytes 884744 | tf_op jit(solution)/shard_map/ppermute | solution.py:41
  86.7 18.9 %collective-permute-start.32 = (bf16[4,48,768]{2,1,0:T(8,128)(2,1)}, bf16[4,48,768]{2,1,0:T(8,128)(2,1)S(1)}, u32[]{:S(2)}, u32[]{:S(2)}) collective-permute-start(bf16[4,48,768]{2,1,0:T(8,128)(2,1)} %get-tuple-element.121.refs_0_), channel_id=1, source_target_pairs={{0,4},{1,5},{2,6},{3,7},{4,0},{5,1},{6,2},{7,3},{8,12},{9,13},{10,... | collective-permute-start | bytes 884744 | tf_op jit(solution)/shard_map/ppermute | solution.py:41
  93.0 15.2 %collective-permute-start.31 = (bf16[4,48,768]{2,1,0:T(8,128)(2,1)}, bf16[4,48,768]{2,1,0:T(8,128)(2,1)S(1)}, u32[]{:S(2)}, u32[]{:S(2)}) collective-permute-start(bf16[4,48,768]{2,1,0:T(8,128)(2,1)} %get-tuple-element.121.refs_0_), channel_id=1, source_target_pairs={{0,2},{1,3},{2,0},{3,1},{4,6},{5,7},{6,4},{7,5},{8,10},{9,11},{10,... | collective-permute-start | bytes 884744 | tf_op jit(solution)/shard_map/ppermute | solution.py:41
  93.5 17.1 %collective-permute-start.35 = (bf16[4,48,768]{2,1,0:T(8,128)(2,1)}, bf16[4,48,768]{2,1,0:T(8,128)(2,1)S(1)}, u32[]{:S(2)}, u32[]{:S(2)}) collective-permute-start(bf16[4,48,768]{2,1,0:T(8,128)(2,1)} %get-tuple-element.122.refs_4_), channel_id=1, source_target_pairs={{0,2},{1,3},{2,0},{3,1},{4,6},{5,7},{6,4},{7,5},{8,10},{9,11},{10,... | collective-permute-start | bytes 884744 | tf_op jit(solution)/shard_map/ppermute | solution.py:41
  99.4 18.9 %collective-permute-start.13 = (bf16[4,48,768]{2,1,0:T(8,128)(2,1)S(1)}, bf16[4,48,768]{2,1,0:T(8,128)(2,1)S(1)}, u32[]{:S(2)}, u32[]{:S(2)}) collective-permute-start(bf16[4,48,768]{2,1,0:T(8,128)(2,1)S(1)} %collective-permute-done.11.refs_1_), channel_id=1, source_target_pairs={{0,4},{1,5},{2,6},{3,7},{4,0},{5,1},{6,2},{7,3},{8,12},{9,13},{10,... | collective-permute-start | bytes 884744 | tf_op jit(solution)/shard_map/ppermute | solution.py:41
  105.6 14.2 %collective-permute-start.16 = (bf16[4,48,768]{2,1,0:T(8,128)(2,1)S(1)}, bf16[4,48,768]{2,1,0:T(8,128)(2,1)S(1)}, u32[]{:S(2)}, u32[]{:S(2)}) collective-permute-start(bf16[4,48,768]{2,1,0:T(8,128)(2,1)S(1)} %collective-permute-done.14.refs_5_), channel_id=1, source_target_pairs={{0,2},{1,3},{2,0},{3,1},{4,6},{5,7},{6,4},{7,5},{8,10},{9,11},{10,... | collective-permute-start | bytes 884744 | tf_op jit(solution)/shard_map/ppermute | solution.py:41
  108.2 16.8 %collective-permute-start.42 = (bf16[4,48,768]{2,1,0:T(8,128)(2,1)}, bf16[4,48,768]{2,1,0:T(8,128)(2,1)S(1)}, u32[]{:S(2)}, u32[]{:S(2)}) collective-permute-start(bf16[4,48,768]{2,1,0:T(8,128)(2,1)} %get-tuple-element.125.refs_0_), channel_id=1, source_target_pairs={{0,4},{1,5},{2,6},{3,7},{4,0},{5,1},{6,2},{7,3},{8,12},{9,13},{10,... | collective-permute-start | bytes 884744 | tf_op jit(solution)/shard_map/ppermute | solution.py:41
  110.7 14.4 %collective-permute-start.41 = (bf16[4,48,768]{2,1,0:T(8,128)(2,1)}, bf16[4,48,768]{2,1,0:T(8,128)(2,1)S(1)}, u32[]{:S(2)}, u32[]{:S(2)}) collective-permute-start(bf16[4,48,768]{2,1,0:T(8,128)(2,1)} %get-tuple-element.125.refs_0_), channel_id=1, source_target_pairs={{0,2},{1,3},{2,0},{3,1},{4,6},{5,7},{6,4},{7,5},{8,10},{9,11},{10,... | collective-permute-start | bytes 884744 | tf_op jit(solution)/shard_map/ppermute | solution.py:41
  112.2 15.6 %collective-permute-start.23 = (bf16[4,48,768]{2,1,0:T(8,128)(2,1)S(1)}, bf16[4,48,768]{2,1,0:T(8,128)(2,1)S(1)}, u32[]{:S(2)}, u32[]{:S(2)}) collective-permute-start(bf16[4,48,768]{2,1,0:T(8,128)(2,1)S(1)} %collective-permute-done.21.refs_1_), channel_id=1, source_target_pairs={{0,4},{1,5},{2,6},{3,7},{4,0},{5,1},{6,2},{7,3},{8,12},{9,13},{10,... | collective-permute-start | bytes 884744 | tf_op jit(solution)/shard_map/ppermute | solution.py:41
  118.3 15.5 %collective-permute-start.44 = (bf16[4,48,768]{2,1,0:T(8,128)(2,1)}, bf16[4,48,768]{2,1,0:T(8,128)(2,1)S(1)}, u32[]{:S(2)}, u32[]{:S(2)}) collective-permute-start(bf16[4,48,768]{2,1,0:T(8,128)(2,1)} %get-tuple-element.126.refs_4_), channel_id=1, source_target_pairs={{0,4},{1,5},{2,6},{3,7},{4,0},{5,1},{6,2},{7,3},{8,12},{9,13},{10,... | collective-permute-start | bytes 884744 | tf_op jit(solution)/shard_map/ppermute | solution.py:41
  125.0 63.2 %collective-permute-start.17 = (bf16[2,16,48,768]{3,2,1,0:T(8,128)(2,1)}, bf16[2,16,48,768]{3,2,1,0:T(8,128)(2,1)}, u32[]{:S(2)}, u32[]{:S(2)}) collective-permute-start(bf16[2,16,48,768]{3,2,1,0:T(8,128)(2,1)} %shard_map.324), channel_id=1, source_target_pairs={{0,1},{1,0},{2,3},{3,2},{4,5},{5,4},{6,7},{7,6},{8,9},{9,8},{10,11... | collective-permute-start | bytes 7077896 | tf_op jit(solution)/shard_map/ppermute | solution.py:47
  128.4 15.7 %collective-permute-start.45 = (bf16[4,48,768]{2,1,0:T(8,128)(2,1)S(1)}, bf16[4,48,768]{2,1,0:T(8,128)(2,1)S(1)}, u32[]{:S(2)}, u32[]{:S(2)}) collective-permute-start(bf16[4,48,768]{2,1,0:T(8,128)(2,1)S(1)} %copy-done.21), channel_id=1, source_target_pairs={{0,2},{1,3},{2,0},{3,1},{4,6},{5,7},{6,4},{7,5},{8,10},{9,11},{10,... | collective-permute-start | bytes 884744 | tf_op jit(solution)/shard_map/ppermute | solution.py:41
  133.8 69.2 %collective-permute-start.27 = (bf16[2,16,48,768]{3,2,1,0:T(8,128)(2,1)}, bf16[2,16,48,768]{3,2,1,0:T(8,128)(2,1)}, u32[]{:S(2)}, u32[]{:S(2)}) collective-permute-start(bf16[2,16,48,768]{3,2,1,0:T(8,128)(2,1)} %shard_map.327), channel_id=1, source_target_pairs={{0,1},{1,0},{2,3},{3,2},{4,5},{5,4},{6,7},{7,6},{8,9},{9,8},{10,11... | collective-permute-start | bytes 7077896 | tf_op jit(solution)/shard_map/ppermute | solution.py:47
  144.1 74.2 %collective-permute-start.37 = (bf16[2,16,48,768]{3,2,1,0:T(8,128)(2,1)}, bf16[2,16,48,768]{3,2,1,0:T(8,128)(2,1)S(1)}, u32[]{:S(2)}, u32[]{:S(2)}) collective-permute-start(bf16[2,16,48,768]{3,2,1,0:T(8,128)(2,1)} %shard_map.330), channel_id=1, source_target_pairs={{0,1},{1,0},{2,3},{3,2},{4,5},{5,4},{6,7},{7,6},{8,9},{9,8},{10,11... | collective-permute-start | bytes 7077896 | tf_op jit(solution)/shard_map/ppermute | solution.py:47
  153.8 79.6 %collective-permute-start.47 = (bf16[2,16,48,768]{3,2,1,0:T(8,128)(2,1)}, bf16[2,16,48,768]{3,2,1,0:T(8,128)(2,1)}, u32[]{:S(2)}, u32[]{:S(2)}) collective-permute-start(bf16[2,16,48,768]{3,2,1,0:T(8,128)(2,1)} %shard_map.333.refs_0_), channel_id=1, source_target_pairs={{0,1},{1,0},{2,3},{3,2},{4,5},{5,4},{6,7},{7,6},{8,9},{9,8},{10,11... | collective-permute-start | bytes 7077896 | tf_op jit(solution)/shard_map/ppermute | solution.py:47
  188.1 57.4 %collective-permute-start.58 = (bf16[2,16,48,384]{3,2,1,0:T(8,128)(2,1)}, bf16[2,16,48,384]{3,2,1,0:T(8,128)(2,1)}, u32[]{:S(2)}, u32[]{:S(2)}) collective-permute-start(bf16[2,16,48,384]{3,2,1,0:T(8,128)(2,1)} %shard_map.336), channel_id=1, source_target_pairs={{0,1},{1,0},{2,3},{3,2},{4,5},{5,4},{6,7},{7,6},{8,9},{9,8},{10,11... | collective-permute-start | bytes 3538952 | tf_op jit(solution)/shard_map/ppermute | solution.py:47
  266.2 130.2 %collective-permute-start.112 = (bf16[2,16,48,384]{3,2,1,0:T(8,128)(2,1)}, bf16[2,16,48,384]{3,2,1,0:T(8,128)(2,1)S(1)}, u32[]{:S(2)}, u32[]{:S(2)}) collective-permute-start(bf16[2,16,48,384]{3,2,1,0:T(8,128)(2,1)} %bitcast.368), channel_id=1, source_target_pairs={{0,1},{1,0},{2,3},{3,2},{4,5},{5,4},{6,7},{7,6},{8,9},{9,8},{10,11... | collective-permute-start | bytes 3538952 | tf_op jit(solution)/shard_map/ppermute | solution.py:47
  393.8 34.0 %collective-permute-start.60 = (bf16[256,768]{1,0:T(8,128)(2,1)}, bf16[256,768]{1,0:T(8,128)(2,1)}, u32[]{:S(2)}, u32[]{:S(2)}) collective-permute-start(bf16[256,768]{1,0:T(8,128)(2,1)} %get-tuple-element.152), channel_id=1, source_target_pairs={{0,8},{1,9},{2,10},{3,11},{4,12},{5,13},{6,14},{7,15},{8,0},{9,1},... | collective-permute-start | bytes 1179656 | tf_op jit(solution)/shard_map/ppermute | solution.py:41
  393.8 60.1 %collective-permute-start.62 = (bf16[2,16,48,768]{3,2,1,0:T(8,128)(2,1)}, bf16[2,16,48,768]{3,2,1,0:T(8,128)(2,1)}, u32[]{:S(2)}, u32[]{:S(2)}) collective-permute-start(bf16[2,16,48,768]{3,2,1,0:T(8,128)(2,1)} %bitcast.367), channel_id=1, source_target_pairs={{0,1},{1,0},{2,3},{3,2},{4,5},{5,4},{6,7},{7,6},{8,9},{9,8},{10,11... | collective-permute-start | bytes 7077896 | tf_op jit(solution)/shard_map/ppermute | solution.py:47
  396.4 63.9 %collective-permute-start.79 = (bf16[2,16,48,768]{3,2,1,0:T(8,128)(2,1)}, bf16[2,16,48,768]{3,2,1,0:T(8,128)(2,1)S(1)}, u32[]{:S(2)}, u32[]{:S(2)}) collective-permute-start(bf16[2,16,48,768]{3,2,1,0:T(8,128)(2,1)} %bitcast.366), channel_id=1, source_target_pairs={{0,1},{1,0},{2,3},{3,2},{4,5},{5,4},{6,7},{7,6},{8,9},{9,8},{10,11... | collective-permute-start | bytes 7077896 | tf_op jit(solution)/shard_map/ppermute | solution.py:47
  421.7 44.7 %collective-permute-start.90 = (bf16[2,16,48,768]{3,2,1,0:T(8,128)(2,1)}, bf16[2,16,48,768]{3,2,1,0:T(8,128)(2,1)}, u32[]{:S(2)}, u32[]{:S(2)}) collective-permute-start(bf16[2,16,48,768]{3,2,1,0:T(8,128)(2,1)} %bitcast.365), channel_id=1, source_target_pairs={{0,1},{1,0},{2,3},{3,2},{4,5},{5,4},{6,7},{7,6},{8,9},{9,8},{10,11... | collective-permute-start | bytes 7077896 | tf_op jit(solution)/shard_map/ppermute | solution.py:47
  427.8 44.7 %collective-permute-start.101 = (bf16[2,16,48,768]{3,2,1,0:T(8,128)(2,1)}, bf16[2,16,48,768]{3,2,1,0:T(8,128)(2,1)}, u32[]{:S(2)}, u32[]{:S(2)}) collective-permute-start(bf16[2,16,48,768]{3,2,1,0:T(8,128)(2,1)} %get-tuple-element.192), channel_id=1, source_target_pairs={{0,1},{1,0},{2,3},{3,2},{4,5},{5,4},{6,7},{7,6},{8,9},{9,8},{10,11... | collective-permute-start | bytes 7077896 | tf_op jit(solution)/shard_map/ppermute | solution.py:47
  458.2 19.5 %collective-permute-start.64 = (bf16[4,48,768]{2,1,0:T(8,128)(2,1)}, bf16[4,48,768]{2,1,0:T(8,128)(2,1)S(1)}, u32[]{:S(2)}, u32[]{:S(2)}) collective-permute-start(bf16[4,48,768]{2,1,0:T(8,128)(2,1)} %get-tuple-element.160), channel_id=1, source_target_pairs={{0,4},{1,5},{2,6},{3,7},{4,0},{5,1},{6,2},{7,3},{8,12},{9,13},{10,... | collective-permute-start | bytes 884744 | tf_op jit(solution)/shard_map/ppermute | solution.py:41
  459.5 19.6 %collective-permute-start.67 = (bf16[4,48,768]{2,1,0:T(8,128)(2,1)}, bf16[4,48,768]{2,1,0:T(8,128)(2,1)S(1)}, u32[]{:S(2)}, u32[]{:S(2)}) collective-permute-start(bf16[4,48,768]{2,1,0:T(8,128)(2,1)} %get-tuple-element.164), channel_id=1, source_target_pairs={{0,2},{1,3},{2,0},{3,1},{4,6},{5,7},{6,4},{7,5},{8,10},{9,11},{10,... | collective-permute-start | bytes 884744 | tf_op jit(solution)/shard_map/ppermute | solution.py:41
  460.3 45.2 %collective-permute-start.63 = (bf16[4,48,768]{2,1,0:T(8,128)(2,1)S(1)}, bf16[4,48,768]{2,1,0:T(8,128)(2,1)S(1)}, u32[]{:S(2)}, u32[]{:S(2)}) collective-permute-start(bf16[4,48,768]{2,1,0:T(8,128)(2,1)S(1)} %copy-done.97), channel_id=1, source_target_pairs={{0,4},{1,5},{2,6},{3,7},{4,0},{5,1},{6,2},{7,3},{8,12},{9,13},{10,... | collective-permute-start | bytes 884744 | tf_op jit(solution)/shard_map/ppermute | solution.py:41
  466.4 46.6 %collective-permute-start.66 = (bf16[4,48,768]{2,1,0:T(8,128)(2,1)S(1)}, bf16[4,48,768]{2,1,0:T(8,128)(2,1)S(1)}, u32[]{:S(2)}, u32[]{:S(2)}) collective-permute-start(bf16[4,48,768]{2,1,0:T(8,128)(2,1)S(1)} %copy-done.95), channel_id=1, source_target_pairs={{0,2},{1,3},{2,0},{3,1},{4,6},{5,7},{6,4},{7,5},{8,10},{9,11},{10,... | collective-permute-start | bytes 884744 | tf_op jit(solution)/shard_map/ppermute | solution.py:41
  472.5 42.8 %collective-permute-start.80 = (bf16[4,48,768]{2,1,0:T(8,128)(2,1)S(1)}, bf16[4,48,768]{2,1,0:T(8,128)(2,1)S(1)}, u32[]{:S(2)}, u32[]{:S(2)}) collective-permute-start(bf16[4,48,768]{2,1,0:T(8,128)(2,1)S(1)} %copy-done.96), channel_id=1, source_target_pairs={{0,4},{1,5},{2,6},{3,7},{4,0},{5,1},{6,2},{7,3},{8,12},{9,13},{10,... | collective-permute-start | bytes 884744 | tf_op jit(solution)/shard_map/ppermute | solution.py:41
  505.5 20.9 %collective-permute-start.83 = (bf16[4,48,768]{2,1,0:T(8,128)(2,1)S(1)}, bf16[4,48,768]{2,1,0:T(8,128)(2,1)S(1)}, u32[]{:S(2)}, u32[]{:S(2)}) collective-permute-start(bf16[4,48,768]{2,1,0:T(8,128)(2,1)S(1)} %copy-done.94), channel_id=1, source_target_pairs={{0,2},{1,3},{2,0},{3,1},{4,6},{5,7},{6,4},{7,5},{8,10},{9,11},{10,... | collective-permute-start | bytes 884744 | tf_op jit(solution)/shard_map/ppermute | solution.py:41
  513.0 14.9 %collective-permute-start.91 = (bf16[4,48,768]{2,1,0:T(8,128)(2,1)S(1)}, bf16[4,48,768]{2,1,0:T(8,128)(2,1)S(1)}, u32[]{:S(2)}, u32[]{:S(2)}) collective-permute-start(bf16[4,48,768]{2,1,0:T(8,128)(2,1)S(1)} %copy-done.93), channel_id=1, source_target_pairs={{0,4},{1,5},{2,6},{3,7},{4,0},{5,1},{6,2},{7,3},{8,12},{9,13},{10,... | collective-permute-start | bytes 884744 | tf_op jit(solution)/shard_map/ppermute | solution.py:41
  515.3 23.0 %collective-permute-start.94 = (bf16[4,48,768]{2,1,0:T(8,128)(2,1)S(1)}, bf16[4,48,768]{2,1,0:T(8,128)(2,1)S(1)}, u32[]{:S(2)}, u32[]{:S(2)}) collective-permute-start(bf16[4,48,768]{2,1,0:T(8,128)(2,1)S(1)} %copy-done.92), channel_id=1, source_target_pairs={{0,2},{1,3},{2,0},{3,1},{4,6},{5,7},{6,4},{7,5},{8,10},{9,11},{10,... | collective-permute-start | bytes 884744 | tf_op jit(solution)/shard_map/ppermute | solution.py:41
  524.7 16.9 %collective-permute-start.102 = (bf16[4,48,768]{2,1,0:T(8,128)(2,1)S(1)}, bf16[4,48,768]{2,1,0:T(8,128)(2,1)S(1)}, u32[]{:S(2)}, u32[]{:S(2)}) collective-permute-start(bf16[4,48,768]{2,1,0:T(8,128)(2,1)S(1)} %copy-done.91), channel_id=1, source_target_pairs={{0,4},{1,5},{2,6},{3,7},{4,0},{5,1},{6,2},{7,3},{8,12},{9,13},{10,... | collective-permute-start | bytes 884744 | tf_op jit(solution)/shard_map/ppermute | solution.py:41
  528.0 21.3 %collective-permute-start.105 = (bf16[4,48,768]{2,1,0:T(8,128)(2,1)S(1)}, bf16[4,48,768]{2,1,0:T(8,128)(2,1)S(1)}, u32[]{:S(2)}, u32[]{:S(2)}) collective-permute-start(bf16[4,48,768]{2,1,0:T(8,128)(2,1)S(1)} %copy-done.90), channel_id=1, source_target_pairs={{0,2},{1,3},{2,0},{3,1},{4,6},{5,7},{6,4},{7,5},{8,10},{9,11},{10,... | collective-permute-start | bytes 884744 | tf_op jit(solution)/shard_map/ppermute | solution.py:41
  539.2 43.1 %collective-permute-start.69 = (bf16[2,48,768]{2,1,0:T(8,128)(2,1)S(1)}, bf16[2,48,768]{2,1,0:T(8,128)(2,1)S(1)}, u32[]{:S(2)}, u32[]{:S(2)}) collective-permute-start(bf16[2,48,768]{2,1,0:T(8,128)(2,1)S(1)} %get-tuple-element.308), channel_id=1, source_target_pairs={{0,24},{1,25},{2,26},{3,27},{4,28},{5,29},{6,30},{7,31},{8,16},{9,... | collective-permute-start | bytes 442376 | tf_op jit(solution)/shard_map/ppermute | solution.py:41
  549.2 35.5 %collective-permute-start.86 = (bf16[2,48,768]{2,1,0:T(8,128)(2,1)S(1)}, bf16[2,48,768]{2,1,0:T(8,128)(2,1)S(1)}, u32[]{:S(2)}, u32[]{:S(2)}) collective-permute-start(bf16[2,48,768]{2,1,0:T(8,128)(2,1)S(1)} %get-tuple-element.305), channel_id=1, source_target_pairs={{0,24},{1,25},{2,26},{3,27},{4,28},{5,29},{6,30},{7,31},{8,16},{9,... | collective-permute-start | bytes 442376 | tf_op jit(solution)/shard_map/ppermute | solution.py:41
  551.2 17.8 %collective-permute-start.88 = (bf16[2,48,768]{2,1,0:T(8,128)(2,1)S(1)}, bf16[2,48,768]{2,1,0:T(8,128)(2,1)S(1)}, u32[]{:S(2)}, u32[]{:S(2)}) collective-permute-start(bf16[2,48,768]{2,1,0:T(8,128)(2,1)S(1)} %get-tuple-element.306), channel_id=1, source_target_pairs={{0,16},{1,17},{2,18},{3,19},{4,20},{5,21},{6,22},{7,23},{8,24},{9,... | collective-permute-start | bytes 442376 | tf_op jit(solution)/shard_map/ppermute | solution.py:41
  551.8 17.2 %collective-permute-start.87 = (bf16[2,48,768]{2,1,0:T(8,128)(2,1)S(1)}, bf16[2,48,768]{2,1,0:T(8,128)(2,1)S(1)}, u32[]{:S(2)}, u32[]{:S(2)}) collective-permute-start(bf16[2,48,768]{2,1,0:T(8,128)(2,1)S(1)} %get-tuple-element.307), channel_id=1, source_target_pairs={{0,8},{1,9},{2,10},{3,11},{4,12},{5,13},{6,14},{7,15},{8,0},{9,1},... | collective-permute-start | bytes 442376 | tf_op jit(solution)/shard_map/ppermute | solution.py:41
  558.9 26.0 %collective-permute-start.97 = (bf16[2,48,768]{2,1,0:T(8,128)(2,1)S(1)}, bf16[2,48,768]{2,1,0:T(8,128)(2,1)S(1)}, u32[]{:S(2)}, u32[]{:S(2)}) collective-permute-start(bf16[2,48,768]{2,1,0:T(8,128)(2,1)S(1)} %get-tuple-element.302), channel_id=1, source_target_pairs={{0,24},{1,25},{2,26},{3,27},{4,28},{5,29},{6,30},{7,31},{8,16},{9,... | collective-permute-start | bytes 442376 | tf_op jit(solution)/shard_map/ppermute | solution.py:41
  (180 other events, 2171.2 us)
